TPU v7x, 256 devices: a whole 4x4x8 slice. The times are simulated.
256 devices in a mesh: lat: 4 (over z_hi), lon: 32 (over y, x, core), inner: 2 (over z_lo).
Axes of the slice: x: 4, y: 4, z: 8 (z_hi: 4, z_lo: 2; z = z_hi * 2 + z_lo), core: 2. Of those that a mesh axis runs over, the one named last changes fastest.
Arguments:
- tokens: bfloat16 [128, 2048, 512], P(('lat', 'inner'), 'lon'), may hold values from -6 to 6
- offsets: int32 [2], replicated, may hold values from 1 to 7, as said below
- regions: int32 [128, 2048], P(('lat', 'inner'), 'lon'), may hold values from 0 to 2
- norm_gain: float32 [512], replicated, may hold values from 0.25 to 1.75
- w_qkv: bfloat16 [512, 1536], replicated
- w_proj: bfloat16 [512, 512], replicated, may hold values from -0.25 to 0.25
- w_merge: bfloat16 [2048, 1024], replicated, may hold values from -0.125 to 0.125
- coarse_gain: float32 [1024], replicated, may hold values from 0.25 to 1.75
- w_in: bfloat16 [1024, 4096], P('lon', 'inner'), may hold values from -0.1875 to 0.1875
- w_out: bfloat16 [4096, 1024], P('inner', 'lon'), may hold values from -0.09375 to 0.09375
Outputs:
- fine_out: bfloat16 [128, 2048, 512], P(('lat', 'inner'), 'lon')
- coarse_out: bfloat16 [64, 1024, 1024], P(('lat', 'inner'), 'lon')
Inputs may be any that keep to these rules, and one draw needn't show every extreme that they name: One of the two offsets is 7.
All inputs are finite; a program needn't handle non-finite values.
Results may differ from a plain program's by a relative error of at most 0.015.
The roundings to bfloat16 on the way count: a program that leaves them out, or rounds other values in their place, can miss the bound.
Values may be sent and summed in bfloat16 or wider, within the bound.
No kernel may reach another device: no remote copies, remote signals or barrier semaphores. Data moves between devices by JAX's collectives and lax.ppermute only.
A program may use at most 128 MiB of HBM per device.

v0:
```python
import jax
import jax.numpy as jnp
from jax import lax
from jax.sharding import PartitionSpec as P

HEADS = 8
W = 8


def with_halo(block, sides, width):
    for axis, dim in sides:
        count = lax.axis_size(axis)
        forward = [(i, i + 1) for i in range(count - 1)]
        forward.append((count - 1, 0))
        backward = [(target, source) for source, target in forward]
        low = lax.ppermute(
            lax.slice_in_dim(block, block.shape[dim] - width, None, axis=dim), axis, forward
        )
        high = lax.ppermute(lax.slice_in_dim(block, 0, width, axis=dim), axis, backward)
        block = jnp.concatenate([low, block, high], axis=dim)
    return block


def layer_norm(values, gain):
    values = values.astype(jnp.float32)
    center = values - jnp.mean(values, axis=-1, keepdims=True)
    spread = jnp.mean(center * center, axis=-1, keepdims=True)
    return center * lax.rsqrt(spread + 1e-05) * gain


def plain_norm(values):
    values = values.astype(jnp.float32)
    center = values - jnp.mean(values, axis=-1, keepdims=True)
    spread = jnp.mean(center * center, axis=-1, keepdims=True)
    return center * lax.rsqrt(spread + 1e-05)


def to_windows(field):
    row_count = field.shape[0] // W
    col_count = field.shape[1] // W
    rest = field.shape[2:]
    order = (0, 2, 1, 3) + tuple(range(4, 4 + len(rest)))
    shaped = field.reshape((row_count, W, col_count, W) + rest).transpose(order)
    return shaped.reshape((row_count * col_count, W * W) + rest)


def from_windows(blocks, row_count, col_count):
    width = blocks.shape[-1]
    shaped = blocks.reshape(row_count, col_count, W, W, width).transpose(0, 2, 1, 3, 4)
    return shaped.reshape(row_count * W, col_count * W, width)


def attend(packed, labels):
    count = packed.shape[0]
    width = packed.shape[-1] // 3
    queries = packed[..., :width].reshape(count, W * W, HEADS, width // HEADS)
    keys_all = packed[..., width : 2 * width].reshape(count, W * W, HEADS, width // HEADS)
    values_all = packed[..., 2 * width :].reshape(count, W * W, HEADS, width // HEADS)
    scores = jnp.einsum("nqhd,nkhd->nhqk", queries, keys_all, preferred_element_type=jnp.float32)
    scores = scores / jnp.sqrt(jnp.float32(width // HEADS))
    allowed = labels[:, None, :, None] == labels[:, None, None, :]
    scores = jnp.where(allowed, scores, jnp.float32(-1e30))
    scores = scores - jnp.max(scores, axis=-1, keepdims=True)
    weights = jnp.exp(scores)
    probs = (weights / jnp.sum(weights, axis=-1, keepdims=True)).astype(jnp.bfloat16)
    mixed = jnp.einsum("nhqk,nkhd->nqhd", probs, values_all, preferred_element_type=jnp.float32)
    return mixed.reshape(count, W * W, width).astype(jnp.bfloat16)


def coarse_block(normed_rows, in_part, out_part):
    before = jnp.dot(
        normed_rows,
        lax.all_gather(in_part, "lon", axis=0, tiled=True),
        preferred_element_type=jnp.float32,
    )
    hidden = jax.nn.gelu(before, approximate=False).astype(jnp.bfloat16)
    return jnp.dot(
        hidden,
        lax.all_gather(out_part, "lon", axis=1, tiled=True),
        preferred_element_type=jnp.float32,
    )


def on_device(
    tokens, offsets, regions, norm_gain, w_qkv, w_proj, w_merge, coarse_gain, w_in, w_out
):
    lat_rows, lon_cols, width = tokens.shape
    margin = W - 1
    lat_shift = offsets[0]
    lon_shift = offsets[1]
    labels = regions.astype(jnp.bfloat16)
    span_rows = lat_rows + W
    span_cols = lon_cols + W
    wide_tokens, wide_labels = (
        with_halo(tokens, ((("lat", "inner"), 0), ("lon", 1)), margin),
        with_halo(labels, ((("lat", "inner"), 0), ("lon", 1)), margin),
    )
    tile = lax.dynamic_slice(
        wide_tokens, (lat_shift - 1, lon_shift - 1, 0), (span_rows, span_cols, width)
    )
    normed = layer_norm(tile, norm_gain).astype(jnp.bfloat16)
    packed = jnp.dot(normed.reshape(-1, width), w_qkv, preferred_element_type=jnp.float32)
    packed = packed.astype(jnp.bfloat16).reshape(tile.shape[0], tile.shape[1], 3 * width)
    label_tile = lax.dynamic_slice(
        wide_labels, (lat_shift - 1, lon_shift - 1), (span_rows, span_cols)
    )
    mixed = attend(to_windows(packed), to_windows(label_tile))
    mixed = from_windows(mixed, span_rows // W, span_cols // W)
    own_mixed = lax.dynamic_slice(
        mixed, (W - lat_shift, W - lon_shift, 0), (lat_rows, lon_cols, width)
    )
    update = jnp.dot(own_mixed.reshape(-1, width), w_proj, preferred_element_type=jnp.float32)
    fine_out = (tokens.astype(jnp.float32) + update.reshape(lat_rows, lon_cols, width)).astype(
        jnp.bfloat16
    )
    grouped = fine_out.reshape(lat_rows // 2, 2, lon_cols // 2, 2, width).transpose(0, 2, 1, 3, 4)
    grouped = plain_norm(grouped.reshape(-1, 4 * width)).astype(jnp.bfloat16)
    coarse = jnp.dot(grouped, w_merge, preferred_element_type=jnp.float32).astype(jnp.bfloat16)
    coarse_normed = layer_norm(coarse, coarse_gain).astype(jnp.bfloat16)
    paired = lax.all_gather(coarse_normed, "inner", axis=0, tiled=True)
    partial_value = coarse_block(paired, w_in, w_out)
    change = lax.psum_scatter(
        partial_value.astype(jnp.bfloat16), "inner", scatter_dimension=0, tiled=True
    ).astype(jnp.float32)
    coarse_out = (coarse.astype(jnp.float32) + change).astype(jnp.bfloat16)
    return (fine_out, coarse_out.reshape(lat_rows // 2, lon_cols // 2, coarse.shape[-1]))


def solution(mesh):
    placed = (
        P(("lat", "inner"), "lon", None),
        P(),
        P(("lat", "inner"), "lon"),
        P(),
        P(),
        P(),
        P(),
        P(),
        P("lon", "inner"),
        P("inner", "lon"),
    )
    return jax.shard_map(
        on_device,
        mesh=mesh,
        in_specs=placed,
        out_specs=(P(("lat", "inner"), "lon", None), P(("lat", "inner"), "lon", None)),
        check_vma=False,
    )
```

profile of v0, /device:TPU:1, one launch (start us, length us, event | category | flops | bytes accessed | tf_op | source)
XLA Modules:
  0.0 291.9 jit_solution(9437751269872356263)
XLA Ops:
  7.2 0.0 copy-start
  7.2 0.0 all-gather.4.cloned.1.call-start
  7.2 1.3 fusion.83
  8.6 2.5 collective-permute-start
  11.1 4.0 %collective-permute-start.1 = (bf16[7,64,512]{2,1,0:T(8,128)(2,1)S(1)}, bf16[7,64,512]{2,1,0:T(8,128)(2,1)S(1)}, u32[]{:S(2)}, u32[]{:S(2)}) collective-permute-start(bf16[7,64,512]{2,1,0:T(8,128)(2,1)S(1)} %get-tuple-element.9), channel_id=1, source_target_pairs={{1,0},{64,1},{65,64},{128,65},{129,128},{192,129},{193,192},{0,193... | collective-permute-start | bytes 1376264 | tf_op jit(solution)/shard_map/ppermute | solution.py:19
  15.2 0.7 convert_element_type.78
  15.9 2.7 collective-permute-start.5
  18.5 1.3 fusion.86
  25.0 0.3 collective-permute-done.4
  25.4 0.1 fusion.84
  25.4 2.3 collective-permute-start.6
  27.8 0.8 collective-permute-done.6
  28.6 2.6 collective-permute-done.7
  31.2 0.1 fusion.43
  31.3 0.1 copy.16
  31.4 0.1 reshape.131
  31.5 0.1 copy.17
  31.6 0.1 eq.20
  31.8 1.3 constant_dynamic-update-slice_fusion.1
  33.2 0.1 fusion.82
  33.2 0.1 collective-permute-start.2
  33.3 2.0 collective-permute-start.3
  35.4 1.0 broadcast_compare_fusion
  36.4 0.1 collective-permute-done.2
  36.5 2.6 collective-permute-done.3
  39.0 1.6 convert_reduce_fusion
  40.7 1.0 fusion.14
  41.8 1.0 fusion.16
  42.8 3.1 %convolution_convert_fusion = bf16[1728,1536]{1,0:T(8,128)(2,1)S(1)} fusion(bf16[1728,512]{1,0:T(8,128)(2,1)S(1)} %bitcast.48, bf16[512,1536]{1,0:T(8,128)(2,1)S(1)} %copy-done), kind=kOutput, calls=%fused_computation.1 | convolution fusion | flops 2720563200 | bytes 8650752 | tf_op jit(solution)/shard_map/dot_general | solution.py:102
  45.9 0.7 copy.14
  46.6 2.5 fusion.81
  49.1 4.3 %reshape.132 = bf16[27,64,8,64]{3,2,1,0:T(8,128)(2,1)S(1)} reshape(bf16[27,64,512]{2,1,0:T(8,128)(2,1)} %get-tuple-element.4) | data formatting | bytes 3538944 | tf_op jit(solution)/shard_map/reshape | solution.py:56
  53.4 5.6 %reshape.133 = bf16[27,64,8,64]{3,2,1,0:T(8,128)(2,1)} reshape(bf16[27,64,512]{2,1,0:T(8,128)(2,1)} %get-tuple-element.5) | data formatting | bytes 3538944 | tf_op jit(solution)/shard_map/reshape | solution.py:57
  59.0 4.5 %copy.15 = bf16[27,64,512]{1,2,0:T(8,128)(2,1)} copy(bf16[27,64,512]{2,1,0:T(8,128)(2,1)} %get-tuple-element.6) | data formatting | bytes 3538944 | tf_op jit(solution)/shard_map/slice | solution.py:58
  63.5 4.0 %fusion.18 = f32[27,8,64,64]{2,3,1,0:T(8,128)S(1)} fusion(bf16[27,64,8,64]{3,2,1,0:T(8,128)(2,1)} %reshape.133, bf16[27,64,8,64]{3,2,1,0:T(8,128)(2,1)S(1)} %reshape.132), kind=kOutput, calls=%fused_computation.33 | convolution fusion | flops 113246208 | bytes 7077888 | tf_op jit(solution)/shard_map/nqhd,nkhd->nhqk/dot_general | solution.py:59
  67.5 3.0 %fusion.87 = (f32[27,8,64]{2,1,0:T(8,128)S(1)}, f32[27,8,64,64]{2,3,1,0:T(8,128)S(1)}) fusion(f32[27,8,64,64]{2,3,1,0:T(8,128)S(1)} %fusion.18, pred[27,64,64]{1,2,0:T(8,128)(4,1)S(1)} %copy-done.4), kind=kOutput, calls=%fused_computation.126 | output fusion | flops 5308479 | bytes 7243776 | tf_op jit(solution)/shard_map/sub | solution.py:63
  70.5 3.0 %convert_bitcast_fusion = bf16[27,64,8,64]{1,3,2,0:T(8,128)(2,1)} fusion(bf16[27,64,8,64]{1,3,2,0:T(8,128)(2,1)S(1)} %bitcast.47, f32[27,8,64,64]{2,3,1,0:T(8,128)S(1)} %get-tuple-element.18, f32[27,8,64]{2,1,0:T(8,128)S(1)} %get-tuple-element.17), kind=kOutput, calls=%fused_computation.36 | convolution fusion | flops 115900416 | bytes 7133184 | tf_op jit(solution)/shard_map/nhqk,nkhd->nqhd/dot_general | solution.py:66
  73.5 4.9 %copy.21 = bf16[27,64,8,64]{3,2,1,0:T(8,128)(2,1)S(1)} copy(bf16[27,64,8,64]{1,3,2,0:T(8,128)(2,1)} %convert_bitcast_fusion) | data formatting | bytes 3538944 | tf_op jit(solution)/shard_map/convert_element_type | solution.py:67
  78.4 3.1 %convert_element_type.82 = bf16[3,9,8,8,512]{4,3,2,1,0:T(8,128)(2,1)} reshape(bf16[27,64,8,64]{3,2,1,0:T(8,128)(2,1)S(1)} %copy.21) | data formatting | bytes 3538944 | tf_op jit(solution)/shard_map/convert_element_type | solution.py:67
  81.5 1.6 copy.22
  83.1 2.1 add_convert_fusion
  85.3 1.3 reshape.138
  86.6 0.7 fusion.79
  87.3 2.1 copy.34
  89.4 3.9 %multiply_reduce_fusion = f32[8,32]{1,0:T(8,128)S(1)} fusion(f32[8,32]{1,0:T(8,128)S(1)} %broadcast_multiply_fusion.1, f32[8,2,32,2,512]{4,3,2,1,0:T(2,128)S(1)} %reshape.138), kind=kLoop, calls=%fused_computation.46 | loop fusion | flops 1572608 | bytes 2099200 | tf_op jit(solution)/shard_map/reduce_sum | solution.py:34
  93.3 0.1 div.41
  93.4 0.1 rsqrt.29
  93.5 4.0 %reshape.136 = f32[256,2048]{1,0:T(8,128)} reshape(f32[8,32,2,2,512]{4,3,2,1,0:T(2,128)} %bitcast.44) | data formatting | bytes 4194304 | tf_op jit(solution)/shard_map/convert_element_type | solution.py:32
  97.6 4.2 %convert_reduce_fusion.1 = (f32[256]{0:T(256)S(1)}, bf16[256,1024]{1,0:T(8,128)(2,1)S(1)}) fusion(bf16[2048,1024]{1,0:T(8,128)(2,1)} %param.16, f32[256,2048]{1,0:T(8,128)} %reshape.136, f32[256]{0:T(256)S(1)} %rsqrt.29, f32[256]{0:T(256)S(1)} %div.41), kind=kOutput, calls=%fused_computation.53 | convolution fusion | flops 1076100864 | bytes 6818816 | tf_op jit(solution)/shard_map/dot_general | solution.py:118
  101.8 0.3 fusion.34
  102.1 1.1 fusion.36
  103.2 0.0 all-gather.4.cloned.1.call-update
  103.2 0.0 all-gather.6.cloned.1.call-start
  103.2 0.7 all-gather.6.cloned.1.call-update
  104.0 0.0 all-gather.8.cloned.1.call-start
  104.0 0.7 all-gather.8.cloned.1.call-update
  104.7 0.3 reduce-scatter.2.cloned.1.call-start
  105.0 29.2 %all-gather.4.cloned.1.call-done = bf16[512,1024]{1,0:T(8,128)(2,1)} async-done(((bf16[256,1024]{1,0:T(8,128)(2,1)}), bf16[512,1024]{1,0:T(8,128)(2,1)}) %all-gather.4.cloned.1.call-update) | async-done | bytes 1048592 | tf_op jit(solution)/shard_map/all_gather | solution.py:120
  134.2 54.5 %all-gather.6.cloned.1.call-done = bf16[1024,2048]{1,0:T(8,128)(2,1)} async-done(((bf16[32,2048]{1,0:T(8,128)(2,1)}), bf16[1024,2048]{1,0:T(8,128)(2,1)}) %all-gather.6.cloned.1.call-update) | async-done | bytes 4194320 | tf_op jit(solution)/shard_map/all_gather | solution.py:73
  188.7 53.1 %all-gather.8.cloned.1.call-done = bf16[2048,1024]{0,1:T(8,128)(2,1)} async-done(((bf16[2048,32]{0,1:T(8,128)(2,1)}), bf16[2048,1024]{0,1:T(8,128)(2,1)}) %all-gather.8.cloned.1.call-update) | async-done | bytes 4194320 | tf_op jit(solution)/shard_map/all_gather | solution.py:79
  241.8 16.8 %fusion.29 = bf16[512,1024]{1,0:T(8,128)(2,1)} fusion(bf16[2048,1024]{0,1:T(8,128)(2,1)} %all-gather.8.cloned.1.call-done, bf16[512,1024]{1,0:T(8,128)(2,1)} %all-gather.4.cloned.1.call-done, bf16[1024,2048]{1,0:T(8,128)(2,1)} %all-gather.6.cloned.1.call-done), kind=kOutput, calls=%fused_computation.54 | convolution fusion | flops 4363649024 | bytes 10485760 | tf_op jit(solution)/shard_map/dot_general | solution.py:77
  258.6 0.0 reduce-scatter.2.cloned.1.call-update
  258.6 24.6 %reduce-scatter.2.cloned.1.call-done = bf16[256,1024]{1,0:T(8,128)(2,1)} async-done(((bf16[512,1024]{1,0:T(8,128)(2,1)}), bf16[256,1024]{1,0:T(8,128)(2,1)}) %reduce-scatter.2.cloned.1.call-update) | async-done | bytes 524304 | tf_op jit(solution)/shard_map/reduce_scatter | solution.py:122
  283.3 2.0 fusion.37
  (28 shorter events, 0.2 us)
Async XLA Ops:
  7.2 35.6 %copy-start = (bf16[512,1536]{1,0:T(8,128)(2,1)S(1)}, bf16[512,1536]{1,0:T(8,128)(2,1)}, u32[]{:S(2)}) copy-start(bf16[512,1536]{1,0:T(8,128)(2,1)} %param.14) | copy-start | bytes 4718596
  7.2 127.0 %all-gather.4.cloned.1.call-start = ((), (), s32[]{:S(2)}) async-start(), calls=%async_computation.1 | async-start | bytes 1572864 | tf_op jit(solution)/shard_map/all_gather | solution.py:120
  8.6 23.2 %collective-permute-start = (bf16[7,64,512]{2,1,0:T(8,128)(2,1)S(1)}, bf16[7,64,512]{2,1,0:T(8,128)(2,1)S(1)}, u32[]{:S(2)}, u32[]{:S(2)}) collective-permute-start(bf16[7,64,512]{2,1,0:T(8,128)(2,1)S(1)} %get-tuple-element.10), channel_id=1, source_target_pairs={{0,1},{1,64},{64,65},{65,128},{128,129},{129,192},{192,193},{193,0... | collective-permute-start | bytes 1376264 | tf_op jit(solution)/shard_map/ppermute | solution.py:16
  11.1 22.0 %collective-permute-start.1 = (bf16[7,64,512]{2,1,0:T(8,128)(2,1)S(1)}, bf16[7,64,512]{2,1,0:T(8,128)(2,1)S(1)}, u32[]{:S(2)}, u32[]{:S(2)}) collective-permute-start(bf16[7,64,512]{2,1,0:T(8,128)(2,1)S(1)} %get-tuple-element.9), channel_id=1, source_target_pairs={{1,0},{64,1},{65,64},{128,65},{129,128},{192,129},{193,192},{0,193... | collective-permute-start | bytes 1376264 | tf_op jit(solution)/shard_map/ppermute | solution.py:19
  15.9 9.5 %collective-permute-start.4 = (bf16[7,64]{1,0:T(8,128)(2,1)S(1)}, bf16[7,64]{1,0:T(8,128)(2,1)S(1)}, u32[]{:S(2)}, u32[]{:S(2)}) collective-permute-start(bf16[7,64]{1,0:T(8,128)(2,1)S(1)} %get-tuple-element.13), channel_id=1, source_target_pairs={{0,1},{1,64},{64,65},{65,128},{128,129},{129,192},{192,193},{193,0... | collective-permute-start | bytes 2696 | tf_op jit(solution)/shard_map/ppermute | solution.py:16
  15.9 9.5 %collective-permute-start.5 = (bf16[7,64]{1,0:T(8,128)(2,1)S(1)}, bf16[7,64]{1,0:T(8,128)(2,1)S(1)}, u32[]{:S(2)}, u32[]{:S(2)}) collective-permute-start(bf16[7,64]{1,0:T(8,128)(2,1)S(1)} %get-tuple-element.14), channel_id=1, source_target_pairs={{1,0},{64,1},{65,64},{128,65},{129,128},{192,129},{193,192},{0,193... | collective-permute-start | bytes 2696 | tf_op jit(solution)/shard_map/ppermute | solution.py:19
  25.4 3.1 %collective-permute-start.6 = (bf16[30,7]{1,0:T(8,128)(2,1)S(1)}, bf16[30,7]{1,0:T(8,128)(2,1)S(1)}, u32[]{:S(2)}, u32[]{:S(2)}) collective-permute-start(bf16[30,7]{1,0:T(8,128)(2,1)S(1)} %get-tuple-element.12), channel_id=1, source_target_pairs={{0,2},{2,4},{4,6},{6,8},{8,10},{10,12},{12,14},{14,16},{16,18},{18... | collective-permute-start | bytes 1268 | tf_op jit(solution)/shard_map/ppermute | solution.py:16
  27.8 3.4 %collective-permute-start.7 = (bf16[30,7]{1,0:T(8,128)(2,1)S(1)}, bf16[30,7]{1,0:T(8,128)(2,1)S(1)}, u32[]{:S(2)}, u32[]{:S(2)}) collective-permute-start(bf16[30,7]{1,0:T(8,128)(2,1)S(1)} %get-tuple-element.11), channel_id=1, source_target_pairs={{2,0},{4,2},{6,4},{8,6},{10,8},{12,10},{14,12},{16,14},{18,16},{20... | collective-permute-start | bytes 1268 | tf_op jit(solution)/shard_map/ppermute | solution.py:19
  33.1 8.6 %copy-start.6 = (f32[512]{0:T(512)S(1)}, f32[512]{0:T(512)}, u32[]{:S(2)}) copy-start(f32[512]{0:T(512)} %param.13) | copy-start | bytes 6148
  33.2 3.2 %collective-permute-start.2 = (bf16[30,7,512]{2,1,0:T(8,128)(2,1)S(1)}, bf16[30,7,512]{2,1,0:T(8,128)(2,1)S(1)}, u32[]{:S(2)}, u32[]{:S(2)}) collective-permute-start(bf16[30,7,512]{2,1,0:T(8,128)(2,1)S(1)} %get-tuple-element.7), channel_id=1, source_target_pairs={{0,2},{2,4},{4,6},{6,8},{8,10},{10,12},{12,14},{14,16},{16,18},{18... | collective-permute-start | bytes 645128 | tf_op jit(solution)/shard_map/ppermute | solution.py:16
  33.3 5.7 %collective-permute-start.3 = (bf16[30,7,512]{2,1,0:T(8,128)(2,1)S(1)}, bf16[30,7,512]{2,1,0:T(8,128)(2,1)S(1)}, u32[]{:S(2)}, u32[]{:S(2)}) collective-permute-start(bf16[30,7,512]{2,1,0:T(8,128)(2,1)S(1)} %get-tuple-element.8), channel_id=1, source_target_pairs={{2,0},{4,2},{6,4},{8,6},{10,8},{12,10},{14,12},{16,14},{18,16},{20... | collective-permute-start | bytes 645128 | tf_op jit(solution)/shard_map/ppermute | solution.py:19
  63.5 4.0 %copy-start.4 = (pred[27,64,64]{1,2,0:T(8,128)(4,1)S(1)}, pred[27,64,64]{1,2,0:T(8,128)(4,1)}, u32[]{:S(2)}) copy-start(pred[27,64,64]{1,2,0:T(8,128)(4,1)} %broadcast_compare_fusion) | copy-start | bytes 331780
  67.5 3.0 %copy-start.2 = (bf16[27,64,512]{1,2,0:T(8,128)(2,1)S(1)}, bf16[27,64,512]{1,2,0:T(8,128)(2,1)}, u32[]{:S(2)}) copy-start(bf16[27,64,512]{1,2,0:T(8,128)(2,1)} %copy.15) | copy-start | bytes 5308420
  85.3 4.2 %copy-start.3 = (bf16[16,64,512]{2,1,0:T(8,128)(2,1)}, bf16[16,64,512]{2,1,0:T(8,128)(2,1)S(1)}, u32[]{:S(2)}) copy-start(bf16[16,64,512]{2,1,0:T(8,128)(2,1)S(1)} %add_convert_fusion) | copy-start | bytes 3145732
  97.5 4.5 %copy-start.5 = (f32[1024]{0:T(1024)S(1)}, f32[1024]{0:T(1024)}, u32[]{:S(2)}) copy-start(f32[1024]{0:T(1024)} %param.17) | copy-start | bytes 12292
  103.2 85.5 %all-gather.6.cloned.1.call-start = ((), (), s32[]{:S(2)}) async-start(), calls=%async_computation.2 | async-start | bytes 4325376 | tf_op jit(solution)/shard_map/all_gather | solution.py:73
  104.0 137.8 %all-gather.8.cloned.1.call-start = ((), (), s32[]{:S(2)}) async-start(), calls=%async_computation.3 | async-start | bytes 4325376 | tf_op jit(solution)/shard_map/all_gather | solution.py:79
  104.7 178.6 %reduce-scatter.2.cloned.1.call-start = ((), (), s32[]{:S(2)}) async-start(), calls=%async_computation.4 | async-start | bytes 1572864 | tf_op jit(solution)/shard_map/reduce_scatter | solution.py:122
  241.8 43.5 %copy-start.1 = (bf16[512,1536]{1,0:T(8,128)(2,1)S(1)}, bf16[512,1536]{1,0:T(8,128)(2,1)}, u32[]{:S(2)}) copy-start(bf16[512,1536]{1,0:T(8,128)(2,1)} %param.14) | copy-start | bytes 4718596
Sparse Core Ops, SparseCore 0:
  103.3 30.8 all-gather.3
  136.7 51.8 all-gather.5
  191.2 50.5 all-gather.7
  258.8 24.4 reduce-scatter.1
where the time goes:
time: 293 us; the launch traced here: 292 us
  waiting for transfers between devices  169 us (58%)
  local copies, waits for them, and re-layouts  39.4 us (13%)
  matrix products  33.3 us (11%)
  between operations  19.2 us (7%)
  other arithmetic  16.5 us (6%)
  starting transfers between devices  14.1 us (5%)
    all_gather x1, waiting for transfers between devices, coarse_block(): lax.all_gather(in_part, 'lon', axis=0, tiled=True)  54.5 us
    all_gather x1, waiting for transfers between devices, coarse_block(): lax.all_gather(out_part, 'lon', axis=1, tiled=True)  53.1 us
    all_gather x1, waiting for transfers between devices, on_device(): paired = lax.all_gather(coarse_normed, 'inner', axis=0, tiled=True)  29.2 us
    reduce_scatter x1, waiting for transfers between devices, on_device(): lax.psum_scatter(partial_value.astype(jnp.bfloat16), 'inner', scatter_dim...  24.6 us
    dot_general x1, matrix products, coarse_block(): jnp.dot(hidden, lax.all_gather(out_part, 'lon', axis=1, tiled=True), pref...  16.8 us
    ppermute x4, starting transfers between devices, with_halo(): lax.ppermute(lax.slice_in_dim(block, 0, width, axis=dim), axis, backward)  8.75 us
    convert_element_type x2, local copies, waits for them, and re-layouts, attend(): return mixed.reshape(count, W * W, width).astype(jnp.bfloat16)  8 us
    convert_element_type x3, local copies, waits for them, and re-layouts, plain_norm(): values = values.astype(jnp.float32)  7.5 us
  transfers between devices with their start and end apart: 12, of which 9 were waited for; matrix products, arithmetic and copies ran while one was open for 2% of the time, Pallas kernels for 0%

commit v1 on v0

v1 whole, which is shorter than its diff:
```python
import jax
import jax.numpy as jnp
import numpy as np
from jax import lax
from jax.experimental import pallas as pl
from jax.experimental.pallas import tpu as pltpu
from jax.sharding import Mesh, PartitionSpec as P

HEADS = 8
W = 8
ROWS = 16
COLS = 64
C = 512
CC = 1024
BANDS = 3
WINS = 9
F32 = jnp.float32
BF16 = jnp.bfloat16


def dot(a, b, dims=((1,), (0,))):
    return lax.dot_general(a, b, (dims, ((), ())), preferred_element_type=F32)


def norm_rows(values):
    width = values.shape[-1]
    center = values - jnp.sum(values, axis=-1, keepdims=True) * (1.0 / width)
    spread = jnp.sum(center * center, axis=-1, keepdims=True) * (1.0 / width)
    return center * lax.rsqrt(spread + 1e-05)


def fine_kernel(
    offs, own, up, down, left, right, up_c, down_c, own_lab, gain, coarse_gain,
    w_qkv_hbm, w_proj_hbm, w_merge_hbm,
    fine_out, coarse_out, normed_out,
    frame, labels, x_buf, packed, mixed, fine, grouped, w_qkv, w_proj, w_merge, sems,
):
    a = offs[0]
    b = offs[1]
    copies = [
        pltpu.make_async_copy(src, dst, sems.at[i])
        for i, (src, dst) in enumerate(
            ((w_qkv_hbm, w_qkv), (w_proj_hbm, w_proj), (w_merge_hbm, w_merge))
        )
    ]
    for copy in copies:
        copy.start()

    def turned(values, steps):
        return pltpu.roll(values, steps, axis=values.ndim - 2)

    in_turn = 8 - b
    frame[8:24, 0] = turned(left[0 : ROWS * 8, :].astype(F32).reshape(ROWS, 8, C), in_turn)
    frame[8:24, 9] = turned(right[0 : ROWS * 8, :].astype(F32).reshape(ROWS, 8, C), in_turn)
    up_v = turned(up_c[0:112, :].astype(F32).reshape(2, 7, 8, C), in_turn)
    frame[1:8, 0] = up_v[0]
    frame[1:8, 9] = up_v[1]
    down_v = turned(down_c[0:112, :].astype(F32).reshape(2, 7, 8, C), in_turn)
    frame[24:31, 0] = down_v[0]
    frame[24:31, 9] = down_v[1]

    @pl.loop(0, ROWS)
    def _(r):
        frame[8 + r, 1:9] = turned(own[r].astype(F32).reshape(8, 8, C), in_turn)

    @pl.loop(0, 7)
    def _(r):
        at = pl.multiple_of(r * COLS, COLS)
        frame[1 + r, 1:9] = turned(up[pl.ds(at, COLS), :].astype(F32).reshape(8, 8, C), in_turn)
        frame[24 + r, 1:9] = turned(
            down[pl.ds(at, COLS), :].astype(F32).reshape(8, 8, C), in_turn
        )

    labels[8:24, :] = (
        own_lab[...].astype(F32)
        + left[128:144, 0:128].astype(F32)
        + right[128:144, 0:128].astype(F32)
    )
    labels[0:8, :] = (up[448:464, 0:128].astype(F32) + up_c[112:128, 0:128].astype(F32))[8:16]
    labels[24:32, :] = (down[448:464, 0:128].astype(F32) + down_c[112:128, 0:128].astype(F32))[0:8]

    gain_v = gain[...]
    lane = lax.broadcasted_iota(jnp.int32, (64, 128), 1)
    inner_col = lax.broadcasted_iota(jnp.int32, (64, 128), 0) % 8
    low_half = lane < 64
    sub = lax.broadcasted_iota(jnp.int32, (8, 8, C), 1)
    copies[0].wait()

    @pl.loop(0, BANDS)
    def _(band):
        row = a + 8 * band

        for w in range(WINS):
            tile = jnp.where(
                sub < 8 - b, frame[pl.ds(row, 8), w], frame[pl.ds(row, 8), w + 1]
            ).reshape(64, C)
            x_buf[64 * w : 64 * w + 64, :] = (norm_rows(tile) * gain_v).astype(BF16)

        for n in range(6):
            packed[:, 256 * n : 256 * n + 256] = dot(
                x_buf[...], w_qkv[:, 256 * n : 256 * n + 256]
            ).astype(BF16)

        band_labels = labels[pl.ds(row, 8), :]
        spread = jnp.broadcast_to(band_labels[:, None, :], (8, 8, 128)).reshape(64, 128)

        @pl.loop(0, WINS)
        def _(w):
            base = pl.multiple_of(w * 64, 64)
            label = jnp.sum(
                jnp.where(lane == inner_col + (8 * w + b), spread, 0.0), axis=-1, keepdims=True
            )
            one = jnp.where(lane == 1, 1.0, 0.0)
            left_side = jnp.where(lane == 0, label, one).astype(BF16)
            right_side = jnp.where(lane == 0, 1.0, jnp.where(lane == 1, -label, 0.0)).astype(BF16)
            differ = dot(left_side, jnp.concatenate([right_side, right_side], axis=0), ((1,), (1,)))
            allowed = differ == 0.0
            outs = []
            for pair in range(HEADS // 2):
                q = packed[pl.ds(base, 64), 128 * pair : 128 * pair + 128]
                k = packed[pl.ds(base, 64), C + 128 * pair : C + 128 * pair + 128]
                v = packed[pl.ds(base, 64), 2 * C + 128 * pair : 2 * C + 128 * pair + 128]
                zero = jnp.zeros_like(q)
                both = jnp.concatenate(
                    [jnp.where(low_half, q, zero), jnp.where(low_half, zero, q)], axis=0
                )
                scores = dot(k, both, ((1,), (1,))) * 0.125
                scores = jnp.where(allowed, scores, -1e30)
                scores = scores - jnp.max(scores, axis=0, keepdims=True)
                weights = jnp.exp(scores)
                total = jnp.sum(weights, axis=0, keepdims=True)
                probs = (weights * (1.0 / total)).astype(BF16)
                result = dot(probs, v, ((0,), (0,)))
                outs.append(jnp.where(low_half, result[:64], result[64:]))
            rows = jnp.concatenate(outs, axis=-1)
            mixed[pl.ds(8 * band, 8), w] = turned(rows.reshape(8, 8, C), b)

    copies[1].wait()
    out_sub = lax.broadcasted_iota(jnp.int32, (4, 8, 8, C), 2)

    @pl.loop(0, ROWS // 4)
    def _(i):
        r = 4 * i
        across = mixed[pl.ds(8 - a + r, 4)]
        mine = jnp.where(out_sub < b, across[:, :8], across[:, 1:])
        mine = mine.reshape(4 * COLS, C).astype(BF16)
        update = dot(mine, w_proj[...])
        value = own[pl.ds(r, 4)].astype(F32).reshape(4 * COLS, C) + update
        rounded = value.astype(BF16)
        fine_out[pl.ds(r, 4)] = rounded.reshape(4, COLS, C)
        exact = rounded.astype(F32)
        for t in range(4):
            fine[t, pl.ds(r, 4)] = exact[:, 128 * t : 128 * t + 128].reshape(4, COLS, 128)

    @pl.loop(0, ROWS // 2)
    def _(i):
        parts = [
            fine[t, 2 * i + dr, pl.ds(dc, COLS // 2, stride=2), :]
            for dr in range(2)
            for dc in range(2)
            for t in range(4)
        ]
        joined = norm_rows(jnp.concatenate(parts, axis=-1))
        grouped[pl.ds(pl.multiple_of(i * 32, 32), 32), :] = joined.astype(BF16)

    copies[2].wait()
    for n in range(4):
        coarse_out[:, 256 * n : 256 * n + 256] = dot(
            grouped[...], w_merge[:, 256 * n : 256 * n + 256]
        ).astype(BF16)
    normed_out[...] = (norm_rows(coarse_out[...].astype(F32)) * coarse_gain[...]).astype(BF16)


def fine_level(offs, own, up, down, left, right, up_c, down_c, own_lab, gain, coarse_gain,
               w_qkv, w_proj, w_merge):
    vmem = pl.BlockSpec(memory_space=pltpu.VMEM)
    anywhere = pl.BlockSpec(memory_space=pl.ANY)
    return pl.pallas_call(
        fine_kernel,
        out_shape=(
            jax.ShapeDtypeStruct((ROWS, COLS, C), BF16),
            jax.ShapeDtypeStruct((256, CC), BF16),
            jax.ShapeDtypeStruct((256, CC), BF16),
        ),
        in_specs=[pl.BlockSpec(memory_space=pltpu.SMEM)] + [vmem] * 10 + [anywhere] * 3,
        out_specs=(vmem, vmem, vmem),
        scratch_shapes=[
            pltpu.VMEM((32, 10, 8, C), F32),
            pltpu.VMEM((32, 128), F32),
            pltpu.VMEM((WINS * 64, C), BF16),
            pltpu.VMEM((WINS * 64, 3 * C), BF16),
            pltpu.VMEM((24, WINS, 8, C), F32),
            pltpu.VMEM((4, ROWS, COLS, 128), F32),
            pltpu.VMEM((256, 4 * C), BF16),
            pltpu.VMEM((C, 3 * C), BF16),
            pltpu.VMEM((C, C), BF16),
            pltpu.VMEM((4 * C, CC), BF16),
            pltpu.SemaphoreType.DMA((3,)),
        ],
        compiler_params=pltpu.CompilerParams(vmem_limit_bytes=50 * 1024 * 1024),
        cost_estimate=pl.CostEstimate(
            flops=9_000_000_000, bytes_accessed=12_000_000, transcendentals=1_000_000
        ),
    )(offs, own, up, down, left, right, up_c, down_c, own_lab, gain, coarse_gain,
      w_qkv, w_proj, w_merge)


def coarse_kernel(x, w_in, w_out, out, acc):
    step = pl.program_id(0)

    @pl.when(step == 0)
    def _():
        acc[...] = jnp.zeros_like(acc)

    width = w_in.shape[-1]
    before = dot(x[...], w_in[...].reshape(CC, width))
    hidden = (0.5 * before * (1.0 + lax.erf(before * np.float32(np.sqrt(0.5))))).astype(BF16)
    acc[...] += dot(hidden, w_out[...].reshape(CC, width), ((1,), (1,)))

    @pl.when(step == pl.num_programs(0) - 1)
    def _():
        out[...] = acc[...].astype(out.dtype)


def coarse_level(x, weights, dtype):
    shards, _, depth, width = weights.shape
    block = 256
    return pl.pallas_call(
        coarse_kernel,
        grid=(width // block,),
        out_shape=jax.ShapeDtypeStruct(x.shape, dtype),
        in_specs=[
            pl.BlockSpec(x.shape, lambda n: (0, 0)),
            pl.BlockSpec((shards, 1, depth, block), lambda n: (0, 0, 0, n)),
            pl.BlockSpec((shards, 1, depth, block), lambda n: (0, 1, 0, n)),
        ],
        out_specs=pl.BlockSpec(x.shape, lambda n: (0, 0)),
        scratch_shapes=[pltpu.VMEM(x.shape, F32)],
        compiler_params=pltpu.CompilerParams(vmem_limit_bytes=40 * 1024 * 1024),
        cost_estimate=pl.CostEstimate(
            flops=4 * x.shape[0] * CC * width, bytes_accessed=10_000_000, transcendentals=0
        ),
    )(x, weights, weights)


def ring(count, step):
    return [(i, (i + step) % count) for i in range(count)]


def on_device(
    tokens, offsets, regions, norm_gain, w_qkv, w_proj, w_merge, coarse_gain, w_in, w_out
):
    rows_axes, rows_n = ("lat", "inner"), lax.axis_size(("lat", "inner"))
    cols_axes, cols_n = ("y", "x", "core"), lax.axis_size(("y", "x", "core"))
    shards = jnp.stack([w_in, w_out.T])
    weights = lax.all_gather(shards, cols_axes, axis=0, tiled=False)

    lab = regions.astype(BF16)
    own_lab = jnp.pad(lab, ((0, 0), (8, 56)))
    wide_lab = jnp.pad(own_lab, ((0, 0), (0, C - 128)))
    to_next = jnp.concatenate([tokens[9:].reshape(-1, C), wide_lab])
    to_prev = jnp.concatenate([tokens[:7].reshape(-1, C), wide_lab])
    to_right = jnp.concatenate(
        [tokens[:, 56:].reshape(-1, C), jnp.pad(lab[:, 56:], ((0, 0), (0, C - 8)))]
    )
    to_left = jnp.concatenate(
        [tokens[:, :8].reshape(-1, C), jnp.pad(lab[:, :8], ((0, 0), (72, C - 80)))]
    )
    left = lax.ppermute(to_right, cols_axes, ring(cols_n, 1))
    right = lax.ppermute(to_left, cols_axes, ring(cols_n, -1))
    up = lax.ppermute(to_next, rows_axes, ring(rows_n, 1))
    down = lax.ppermute(to_prev, rows_axes, ring(rows_n, -1))
    side_lab = left[128:] + right[128:]
    up_c = lax.ppermute(
        jnp.concatenate([left[72:128], right[72:128], side_lab]), rows_axes, ring(rows_n, 1)
    )
    down_c = lax.ppermute(
        jnp.concatenate([left[:56], right[:56], side_lab]), rows_axes, ring(rows_n, -1)
    )
    fine_out, coarse, normed = fine_level(
        offsets, tokens, up, down, left, right, up_c, down_c, own_lab,
        norm_gain.reshape(1, -1), coarse_gain.reshape(1, -1), w_qkv, w_proj, w_merge,
    )
    swap = [(0, 1), (1, 0)]
    theirs = lax.ppermute(normed, "inner", swap)
    their_part = coarse_level(theirs, weights, BF16)
    returned = lax.ppermute(their_part, "inner", swap)
    own_part = coarse_level(normed, weights, F32)
    coarse_out = (coarse.astype(F32) + own_part + returned.astype(F32)).astype(BF16)
    return fine_out, coarse_out.reshape(ROWS // 2, COLS // 2, CC)


def solution(mesh):
    fine_mesh = Mesh(
        np.array(mesh.devices).reshape(4, 4, 4, 2, 2), ("lat", "y", "x", "core", "inner")
    )
    lon = ("y", "x", "core")
    placed = (
        P(("lat", "inner"), lon, None),
        P(),
        P(("lat", "inner"), lon),
        P(),
        P(),
        P(),
        P(),
        P(),
        P(lon, "inner"),
        P("inner", lon),
    )
    return jax.shard_map(
        on_device,
        mesh=fine_mesh,
        in_specs=placed,
        out_specs=(P(("lat", "inner"), lon, None), P(("lat", "inner"), lon, None)),
        check_vma=False,
    )
```

time: 293 us -> 119 us (0.41)
  the two profiles are of different devices: /device:TPU:1 before, /device:TPU:6 now
where the time goes in v1:
time: 119 us; the launch traced here: 118 us
  Pallas kernels  53.4 us (45%)
  waiting for transfers between devices  29.7 us (25%)
  between operations  14.2 us (12%)
  starting transfers between devices  11.6 us (10%)
  local copies, waits for them, and re-layouts  5.79 us (5%)
  other arithmetic  3.67 us (3%)
    pallas_call x1, Pallas kernels, fine_level(): pl.pallas_call(fine_kernel, out_shape=(jax.ShapeDtypeStruct((ROWS, COLS,...  38.7 us
    pallas_call x2, Pallas kernels, coarse_level(): pl.pallas_call(coarse_kernel, grid=(width // block,), out_shape=jax.Shape...  14.7 us
    ppermute x1, waiting for transfers between devices, on_device(): theirs = lax.ppermute(normed, 'inner', swap)  12.6 us
    ppermute x1, waiting for transfers between devices, on_device(): lax.ppermute(jnp.concatenate([left[:56], right[:56], side_lab]), rows_axe...  9.58 us
    ppermute x1, starting transfers between devices, on_device(): down = lax.ppermute(to_prev, rows_axes, ring(rows_n, -1))  5.93 us
    ppermute x1, waiting for transfers between devices, on_device(): returned = lax.ppermute(their_part, 'inner', swap)  4.07 us
    ppermute x1, waiting for transfers between devices, on_device(): lax.ppermute(jnp.concatenate([left[72:128], right[72:128], side_lab]), ro...  3.41 us
    unnamed x10, local copies, waits for them, and re-layouts  3.4 us
  transfers between devices with their start and end apart: 9, of which 4 were waited for; matrix products, arithmetic and copies ran while one was open for 3% of the time, Pallas kernels for 39%

profile of v1, /device:TPU:6, one launch (start us, length us, event | category | flops | bytes accessed | tf_op | source)
XLA Modules:
  0.0 118.3 jit_solution(14330222055936987686)
XLA Ops:
  7.2 0.0 copy-start.2
  7.2 0.0 copy-start.1
  7.2 0.0 copy-start.3
  7.2 0.0 copy-start.4
  7.2 0.0 all-gather.3.cloned.1.call-start
  7.3 1.7 %pad_maximum_fusion = bf16[2,32,2048]{2,1,0:T(8,128)(2,1)} fusion(bf16[1,32,2048]{2,1,0:T(8,128)(2,1)} %bitcast.23, bf16[1,32,2048]{2,1,0:T(8,128)(2,1)} %bitcast.24), kind=kLoop, calls=%fused_computation.8 | loop fusion | flops 131072 | bytes 524288 | tf_op jit(solution)/shard_map/stack | solution.py:255
  9.0 0.0 all-gather.3.cloned.1.call-update
  9.0 0.7 convert_element_type.20
  9.7 0.1 fusion.10
  9.8 1.0 slice_bitcast_fusion
  10.8 0.1 collective-permute-start.2
  10.9 0.1 fusion.6
  11.0 1.7 %collective-permute-start.3 = (bf16[144,512]{1,0:T(8,128)(2,1)S(1)}, bf16[144,512]{1,0:T(8,128)(2,1)S(1)}, u32[]{:S(2)}, u32[]{:S(2)}) collective-permute-start(bf16[144,512]{1,0:T(8,128)(2,1)S(1)} %fusion.6), channel_id=1, source_target_pairs={{0,62},{2,0},{4,2},{6,4},{8,6},{10,8},{12,10},{14,12},{16,14},{18,... | collective-permute-start | bytes 442376 | tf_op jit(solution)/shard_map/ppermute | solution.py:270
  12.7 1.2 %fusion.7 = (bf16[7,64,512]{2,1,0:T(8,128)(2,1)S(1)}, bf16[7,64,512]{2,1,0:T(8,128)(2,1)S(1)}) fusion(bf16[16,64,512]{2,1,0:T(8,128)(2,1)} %own.1), kind=kLoop, calls=%fused_computation.16 | loop fusion | bytes 1835008 | tf_op jit(solution)/shard_map/slice | solution.py:262
  14.0 0.1 pad.16.own_lab
  14.0 0.1 fusion.2
  14.1 5.9 %collective-permute-start.1 = (bf16[464,512]{1,0:T(8,128)(2,1)S(1)}, bf16[464,512]{1,0:T(8,128)(2,1)S(1)}, u32[]{:S(2)}, u32[]{:S(2)}) collective-permute-start(bf16[464,512]{1,0:T(8,128)(2,1)S(1)} %get-tuple-element.20), channel_id=1, source_target_pairs={{0,193},{1,0},{64,1},{65,64},{128,65},{129,128},{192,129},{193,192... | collective-permute-start | bytes 1425416 | tf_op jit(solution)/shard_map/ppermute | solution.py:272
  20.1 0.0 collective-permute-start
  20.1 0.0 collective-permute-done.2.left
  20.1 0.0 collective-permute-done.3.right
  20.1 3.3 %collective-permute-start.5 = (bf16[128,512]{1,0:T(8,128)(2,1)S(1)}, bf16[128,512]{1,0:T(8,128)(2,1)S(1)}, u32[]{:S(2)}, u32[]{:S(2)}) collective-permute-start(bf16[128,512]{1,0:T(8,128)(2,1)S(1)} %get-tuple-element.16), channel_id=1, source_target_pairs={{0,193},{1,0},{64,1},{65,64},{128,65},{129,128},{192,129},{193,192... | collective-permute-start | bytes 393224 | tf_op jit(solution)/shard_map/ppermute | solution.py:277
  23.5 0.0 collective-permute-start.4
  23.5 9.6 %collective-permute-done.5.down_c = bf16[128,512]{1,0:T(8,128)(2,1)S(1)} collective-permute-done((bf16[128,512]{1,0:T(8,128)(2,1)S(1)}, bf16[128,512]{1,0:T(8,128)(2,1)S(1)}, u32[]{:S(2)}, u32[]{:S(2)}) %collective-permute-start.5) | collective-permute-done | bytes 131104 | tf_op jit(solution)/shard_map/ppermute | solution.py:277
  33.0 3.4 %collective-permute-done.4.up_c = bf16[128,512]{1,0:T(8,128)(2,1)S(1)} collective-permute-done((bf16[128,512]{1,0:T(8,128)(2,1)S(1)}, bf16[128,512]{1,0:T(8,128)(2,1)S(1)}, u32[]{:S(2)}, u32[]{:S(2)}) %collective-permute-start.4) | collective-permute-done | bytes 131104 | tf_op jit(solution)/shard_map/ppermute | solution.py:274
  36.5 0.0 collective-permute-done.1.down
  36.5 0.0 collective-permute-done.up
  36.5 0.0 copy-done.2
  36.5 0.0 copy-done.1
  36.5 0.0 copy-done.3
  36.5 0.0 copy-done.4
  36.5 38.7 %shard_map.113 = (bf16[16,64,512]{2,1,0:T(8,128)(2,1)}, bf16[256,1024]{1,0:T(8,128)(2,1)S(1)}, bf16[256,1024]{1,0:T(8,128)(2,1)S(1)}) custom-call(s32[2]{0:T(128)S(1)} %copy-done.4, bf16[16,64,512]{2,1,0:T(8,128)(2,1)} %own.1, bf16[464,512]{1,0:T(8,128)(2,1)S(1)} %collective-permute-done.up, bf16[464,512]{1,0:T(8,128)(2,1)S(1)} %collective-permute-done.1.down, ...), custom_call_target="tpu_custom_call" | custom-call | flops 8999999488 | bytes 12000000 | tf_op jit(solution)/shard_map/pallas_call | solution.py:178
  75.2 0.1 collective-permute-start.6
  75.3 12.6 %collective-permute-done.6.x = bf16[256,1024]{1,0:T(8,128)(2,1)S(1)} collective-permute-done((bf16[256,1024]{1,0:T(8,128)(2,1)S(1)}, bf16[256,1024]{1,0:T(8,128)(2,1)S(1)}, u32[]{:S(2)}, u32[]{:S(2)}) %collective-permute-start.6) | collective-permute-done | bytes 524320 | tf_op jit(solution)/shard_map/ppermute | solution.py:285
  87.9 0.0 all-gather.3.cloned.1.call-done
  87.9 0.0 copy-start
  87.9 3.4 %copy-done = bf16[64,32,2048]{2,1,0:T(8,128)(2,1)S(1)} copy-done((bf16[64,32,2048]{2,1,0:T(8,128)(2,1)S(1)}, bf16[64,32,2048]{2,1,0:T(8,128)(2,1)}, u32[]{:S(2)}) %copy-start) | copy-done | bytes 8388632
  91.3 7.3 %shard_map.115 = bf16[256,1024]{1,0:T(8,128)(2,1)S(1)} custom-call(bf16[256,1024]{1,0:T(8,128)(2,1)S(1)} %collective-permute-done.6.x, bf16[32,2,32,2048]{3,2,1,0:T(8,128)(2,1)S(1)} %bitcast.14, bf16[32,2,32,2048]{3,2,1,0:T(8,128)(2,1)S(1)} %bitcast.15), custom_call_target="tpu_custom_call" | custom-call | flops 2147483648 | bytes 10000000 | tf_op jit(solution)/shard_map/pallas_call | solution.py:228
  98.6 0.4 collective-permute-start.7
  99.0 7.4 %shard_map.114 = f32[256,1024]{1,0:T(8,128)S(1)} custom-call(bf16[256,1024]{1,0:T(8,128)(2,1)S(1)} %get-tuple-element.7.x, bf16[32,2,32,2048]{3,2,1,0:T(8,128)(2,1)S(1)} %bitcast.16, bf16[32,2,32,2048]{3,2,1,0:T(8,128)(2,1)S(1)} %bitcast.17), custom_call_target="tpu_custom_call" | custom-call | flops 2147483648 | bytes 10000000 | tf_op jit(solution)/shard_map/pallas_call | solution.py:228
  106.4 4.1 %collective-permute-done.7 = bf16[256,1024]{1,0:T(8,128)(2,1)S(1)} collective-permute-done((bf16[256,1024]{1,0:T(8,128)(2,1)S(1)}, bf16[256,1024]{1,0:T(8,128)(2,1)S(1)}, u32[]{:S(2)}, u32[]{:S(2)}) %collective-permute-start.7) | collective-permute-done | bytes 524320 | tf_op jit(solution)/shard_map/ppermute | solution.py:287
  110.4 1.0 add_convert_fusion
  (5 shorter events, 0.1 us)
Async XLA Ops:
  7.2 29.3 %copy-start.2 = (f32[1024]{0:T(1024)S(1)}, f32[1024]{0:T(1024)}, u32[]{:S(2)}) copy-start(f32[1024]{0:T(1024)} %param.17) | copy-start | bytes 12292
  7.2 29.3 %copy-start.1 = (bf16[512,512]{1,0:T(8,128)(2,1)S(1)}, bf16[512,512]{1,0:T(8,128)(2,1)}, u32[]{:S(2)}) copy-start(bf16[512,512]{1,0:T(8,128)(2,1)} %w_proj_hbm.1) | copy-start | bytes 1572868
  7.2 29.3 %copy-start.3 = (f32[512]{0:T(512)S(1)}, f32[512]{0:T(512)}, u32[]{:S(2)}) copy-start(f32[512]{0:T(512)} %param.13) | copy-start | bytes 6148
  7.2 29.3 %copy-start.4 = (s32[2]{0:T(128)S(1)}, s32[2]{0:T(128)}, u32[]{:S(2)}) copy-start(s32[2]{0:T(128)} %offs.1) | copy-start | bytes 28
  7.2 80.7 %all-gather.3.cloned.1.call-start = ((), (), s32[]{:S(2)}) async-start(), calls=%async_computation | async-start | bytes 8650752 | tf_op jit(solution)/shard_map/all_gather | solution.py:256
  10.8 9.3 %collective-permute-start.2 = (bf16[144,512]{1,0:T(8,128)(2,1)S(1)}, bf16[144,512]{1,0:T(8,128)(2,1)S(1)}, u32[]{:S(2)}, u32[]{:S(2)}) collective-permute-start(bf16[144,512]{1,0:T(8,128)(2,1)S(1)} %fusion.5), channel_id=1, source_target_pairs={{0,2},{2,4},{4,6},{6,8},{8,10},{10,12},{12,14},{14,16},{16,18},{18... | collective-permute-start | bytes 442376 | tf_op jit(solution)/shard_map/ppermute | solution.py:269
  11.0 9.1 %collective-permute-start.3 = (bf16[144,512]{1,0:T(8,128)(2,1)S(1)}, bf16[144,512]{1,0:T(8,128)(2,1)S(1)}, u32[]{:S(2)}, u32[]{:S(2)}) collective-permute-start(bf16[144,512]{1,0:T(8,128)(2,1)S(1)} %fusion.6), channel_id=1, source_target_pairs={{0,62},{2,0},{4,2},{6,4},{8,6},{10,8},{12,10},{14,12},{16,14},{18,... | collective-permute-start | bytes 442376 | tf_op jit(solution)/shard_map/ppermute | solution.py:270
  14.1 22.3 %collective-permute-start.1 = (bf16[464,512]{1,0:T(8,128)(2,1)S(1)}, bf16[464,512]{1,0:T(8,128)(2,1)S(1)}, u32[]{:S(2)}, u32[]{:S(2)}) collective-permute-start(bf16[464,512]{1,0:T(8,128)(2,1)S(1)} %get-tuple-element.20), channel_id=1, source_target_pairs={{0,193},{1,0},{64,1},{65,64},{128,65},{129,128},{192,129},{193,192... | collective-permute-start | bytes 1425416 | tf_op jit(solution)/shard_map/ppermute | solution.py:272
  20.1 16.4 %collective-permute-start = (bf16[464,512]{1,0:T(8,128)(2,1)S(1)}, bf16[464,512]{1,0:T(8,128)(2,1)S(1)}, u32[]{:S(2)}, u32[]{:S(2)}) collective-permute-start(bf16[464,512]{1,0:T(8,128)(2,1)S(1)} %get-tuple-element.21), channel_id=1, source_target_pairs={{0,1},{1,64},{64,65},{65,128},{128,129},{129,192},{192,193},{193,0... | collective-permute-start | bytes 1425416 | tf_op jit(solution)/shard_map/ppermute | solution.py:271
  20.1 12.9 %collective-permute-start.5 = (bf16[128,512]{1,0:T(8,128)(2,1)S(1)}, bf16[128,512]{1,0:T(8,128)(2,1)S(1)}, u32[]{:S(2)}, u32[]{:S(2)}) collective-permute-start(bf16[128,512]{1,0:T(8,128)(2,1)S(1)} %get-tuple-element.16), channel_id=1, source_target_pairs={{0,193},{1,0},{64,1},{65,64},{128,65},{129,128},{192,129},{193,192... | collective-permute-start | bytes 393224 | tf_op jit(solution)/shard_map/ppermute | solution.py:277
  23.5 13.0 %collective-permute-start.4 = (bf16[128,512]{1,0:T(8,128)(2,1)S(1)}, bf16[128,512]{1,0:T(8,128)(2,1)S(1)}, u32[]{:S(2)}, u32[]{:S(2)}) collective-permute-start(bf16[128,512]{1,0:T(8,128)(2,1)S(1)} %get-tuple-element.17), channel_id=1, source_target_pairs={{0,1},{1,64},{64,65},{65,128},{128,129},{129,192},{192,193},{193,0... | collective-permute-start | bytes 393224 | tf_op jit(solution)/shard_map/ppermute | solution.py:274
  75.2 12.7 %collective-permute-start.6 = (bf16[256,1024]{1,0:T(8,128)(2,1)S(1)}, bf16[256,1024]{1,0:T(8,128)(2,1)S(1)}, u32[]{:S(2)}, u32[]{:S(2)}) collective-permute-start(bf16[256,1024]{1,0:T(8,128)(2,1)S(1)} %get-tuple-element.7.x), channel_id=1, source_target_pairs={{0,1},{1,0},{2,3},{3,2},{4,5},{5,4},{6,7},{7,6},{8,9},{9,8},{10,11... | collective-permute-start | bytes 1572872 | tf_op jit(solution)/shard_map/ppermute | solution.py:285
  87.9 3.4 %copy-start = (bf16[64,32,2048]{2,1,0:T(8,128)(2,1)S(1)}, bf16[64,32,2048]{2,1,0:T(8,128)(2,1)}, u32[]{:S(2)}) copy-start(bf16[64,32,2048]{2,1,0:T(8,128)(2,1)} %all-gather.3.cloned.1.call-done) | copy-start | bytes 25165828
  98.6 11.8 %collective-permute-start.7 = (bf16[256,1024]{1,0:T(8,128)(2,1)S(1)}, bf16[256,1024]{1,0:T(8,128)(2,1)S(1)}, u32[]{:S(2)}, u32[]{:S(2)}) collective-permute-start(bf16[256,1024]{1,0:T(8,128)(2,1)S(1)} %shard_map.115), channel_id=1, source_target_pairs={{0,1},{1,0},{2,3},{3,2},{4,5},{5,4},{6,7},{7,6},{8,9},{9,8},{10,11... | collective-permute-start | bytes 1572872 | tf_op jit(solution)/shard_map/ppermute | solution.py:287
Sparse Core Ops, SparseCore 0:
  11.2 60.9 all-gather.2

commit v2 on v1

v2 whole, which is shorter than its diff:
```python
import jax
import jax.numpy as jnp
import numpy as np
from jax import lax
from jax.experimental import pallas as pl
from jax.experimental.pallas import tpu as pltpu
from jax.sharding import Mesh, PartitionSpec as P

HEADS = 8
W = 8
ROWS = 16
COLS = 64
C = 512
CC = 1024
BANDS = 3
WINS = 9
GROUP = 3
QUAD = 256
MOST = 62 * 1024 * 1024
F32 = jnp.float32
BF16 = jnp.bfloat16


def dot(a, b, dims=((1,), (0,))):
    return lax.dot_general(a, b, (dims, ((), ())), preferred_element_type=F32)


def norm_rows(values):
    width = values.shape[-1]
    center = values - jnp.sum(values, axis=-1, keepdims=True) * (1.0 / width)
    spread = jnp.sum(center * center, axis=-1, keepdims=True) * (1.0 / width)
    return center * lax.rsqrt(spread + 1e-05)


def fine_kernel(
    offs, up, down, left, right, up_c, down_c, own_lab, own_hbm, gain_hbm, coarse_gain_hbm,
    w_qkv_hbm, w_proj_hbm, w_merge_hbm,
    fine_out, coarse_out, normed_a, normed_b,
    frame, labels, x_buf, packed, mixed, fine, grouped,
    own, gain, coarse_gain, w_qkv, w_proj, w_merge, sems,
):
    a = offs[0]
    b = offs[1]
    copies = [
        pltpu.make_async_copy(src, dst, sems.at[i])
        for i, (src, dst) in enumerate(
            (
                (own_hbm, own),
                (gain_hbm, gain),
                (w_qkv_hbm, w_qkv),
                (w_proj_hbm, w_proj),
                (w_merge_hbm, w_merge),
                (coarse_gain_hbm, coarse_gain),
            )
        )
    ]
    for copy in copies:
        copy.start()

    def turned(values, steps):
        return pltpu.roll(values, steps, axis=values.ndim - 2)

    in_turn = 8 - b
    frame[8:24, 0] = turned(left[0 : ROWS * 8, :].astype(F32).reshape(ROWS, 8, C), in_turn)
    frame[8:24, 9] = turned(right[0 : ROWS * 8, :].astype(F32).reshape(ROWS, 8, C), in_turn)
    up_v = turned(up_c[0:112, :].astype(F32).reshape(2, 7, 8, C), in_turn)
    frame[1:8, 0] = up_v[0]
    frame[1:8, 9] = up_v[1]
    down_v = turned(down_c[0:112, :].astype(F32).reshape(2, 7, 8, C), in_turn)
    frame[24:31, 0] = down_v[0]
    frame[24:31, 9] = down_v[1]

    @pl.loop(0, 7)
    def _(r):
        at = pl.multiple_of(r * COLS, COLS)
        frame[1 + r, 1:9] = turned(up[pl.ds(at, COLS), :].astype(F32).reshape(8, 8, C), in_turn)
        frame[24 + r, 1:9] = turned(
            down[pl.ds(at, COLS), :].astype(F32).reshape(8, 8, C), in_turn
        )

    labels[8:24, :] = (
        own_lab[...].astype(F32)
        + left[128:144, 0:128].astype(F32)
        + right[128:144, 0:128].astype(F32)
    )
    labels[0:8, :] = (up[448:464, 0:128].astype(F32) + up_c[112:128, 0:128].astype(F32))[8:16]
    labels[24:32, :] = (down[448:464, 0:128].astype(F32) + down_c[112:128, 0:128].astype(F32))[0:8]

    copies[0].wait()

    @pl.loop(0, ROWS)
    def _(r):
        frame[8 + r, 1:9] = turned(own[r].astype(F32).reshape(8, 8, C), in_turn)

    copies[1].wait()
    gain_v = gain[...]
    lane = lax.broadcasted_iota(jnp.int32, (64, 128), 1)
    inner_col = lax.broadcasted_iota(jnp.int32, (64, 128), 0) % 8
    low_half = lane < 64
    head_lane = lax.broadcasted_iota(jnp.int32, (64, QUAD), 1) // 64
    sub = lax.broadcasted_iota(jnp.int32, (8, 8, C), 1)
    copies[2].wait()

    @pl.loop(0, BANDS)
    def _(band):
        row = a + 8 * band

        for w in range(WINS):
            tile = jnp.where(
                sub < 8 - b, frame[pl.ds(row, 8), w], frame[pl.ds(row, 8), w + 1]
            ).reshape(64, C)
            x_buf[64 * w : 64 * w + 64, :] = (norm_rows(tile) * gain_v).astype(BF16)

        for n in range(6):
            packed[:, 256 * n : 256 * n + 256] = dot(
                x_buf[...], w_qkv[:, 256 * n : 256 * n + 256]
            ).astype(BF16)

        band_labels = labels[pl.ds(row, 8), :]
        spread = jnp.broadcast_to(band_labels[:, None, :], (8, 8, 128)).reshape(64, 128)

        @pl.loop(0, WINS // GROUP)
        def _(g):
            masks, rows = [], []
            for j in range(GROUP):
                w = GROUP * g + j
                label = jnp.sum(
                    jnp.where(lane == inner_col + (8 * w + b), spread, 0.0), axis=-1, keepdims=True
                )
                one = jnp.where(lane == 1, 1.0, 0.0)
                left_side = jnp.where(lane == 0, label, one).astype(BF16)
                right_side = jnp.where(lane == 0, 1.0, jnp.where(lane == 1, -label, 0.0))
                right_side = right_side.astype(BF16)
                differ = dot(left_side, jnp.concatenate([right_side] * 4, axis=0), ((1,), (1,)))
                masks.append(differ == 0.0)
                rows.append(pl.ds(pl.multiple_of(w * 64, 64), 64))
            all_scores = []
            for j in range(GROUP):
                for part in range(2):
                    q = packed[rows[j], QUAD * part : QUAD * part + QUAD]
                    k = packed[rows[j], C + QUAD * part : C + QUAD * part + QUAD]
                    zero = jnp.zeros_like(q)
                    spread_q = jnp.concatenate(
                        [jnp.where(head_lane == h, q, zero) for h in range(4)], axis=0
                    )
                    all_scores.append(dot(k, spread_q, ((1,), (1,))))
            all_probs = []
            for j in range(GROUP):
                for part in range(2):
                    scores = jnp.where(masks[j], all_scores[2 * j + part] * 0.125, -1e30)
                    scores = scores - jnp.max(scores, axis=0, keepdims=True)
                    weights = jnp.exp(scores)
                    total = jnp.sum(weights, axis=0, keepdims=True)
                    all_probs.append((weights * (1.0 / total)).astype(BF16))
            for j in range(GROUP):
                outs = []
                for part in range(2):
                    v = packed[rows[j], 2 * C + QUAD * part : 2 * C + QUAD * part + QUAD]
                    for half in range(2):
                        result = dot(
                            all_probs[2 * j + part][:, 128 * half : 128 * half + 128],
                            v[:, 128 * half : 128 * half + 128],
                            ((0,), (0,)),
                        )
                        outs.append(jnp.where(low_half, result[:64], result[64:]))
                value = jnp.concatenate(outs, axis=-1)
                mixed[pl.ds(8 * band, 8), GROUP * g + j] = turned(value.reshape(8, 8, C), b)

    copies[3].wait()
    out_sub = lax.broadcasted_iota(jnp.int32, (4, 8, 8, C), 2)

    @pl.loop(0, ROWS // 4)
    def _(i):
        r = 4 * i
        across = mixed[pl.ds(8 - a + r, 4)]
        mine = jnp.where(out_sub < b, across[:, :8], across[:, 1:])
        mine = mine.reshape(4 * COLS, C).astype(BF16)
        update = dot(mine, w_proj[...])
        value = own[pl.ds(r, 4)].astype(F32).reshape(4 * COLS, C) + update
        rounded = value.astype(BF16)
        fine_out[pl.ds(r, 4)] = rounded.reshape(4, COLS, C)
        exact = rounded.astype(F32)
        for t in range(4):
            fine[t, pl.ds(r, 4)] = exact[:, 128 * t : 128 * t + 128].reshape(4, COLS, 128)

    @pl.loop(0, ROWS // 2)
    def _(i):
        parts = [
            fine[t, 2 * i + dr, pl.ds(dc, COLS // 2, stride=2), :]
            for dr in range(2)
            for dc in range(2)
            for t in range(4)
        ]
        joined = norm_rows(jnp.concatenate(parts, axis=-1))
        grouped[pl.ds(pl.multiple_of(i * 32, 32), 32), :] = joined.astype(BF16)

    copies[4].wait()
    for n in range(4):
        coarse_out[:, 256 * n : 256 * n + 256] = dot(
            grouped[...], w_merge[:, 256 * n : 256 * n + 256]
        ).astype(BF16)
    copies[5].wait()
    for part, out in enumerate((normed_a, normed_b)):
        rows = coarse_out[128 * part : 128 * part + 128, :].astype(F32)
        out[...] = (norm_rows(rows) * coarse_gain[...]).astype(BF16)


def pack_kernel(
    tokens, regions, to_next, to_prev, to_right, to_left, own_lab
):
    area = 7 * COLS
    label = regions[...].astype(F32)
    label = jnp.concatenate([label, jnp.zeros((ROWS, 128 - COLS), F32)], axis=-1)
    label = pltpu.roll(label, 8, axis=1)
    lane = lax.broadcasted_iota(jnp.int32, label.shape, 1)
    last = pltpu.roll(jnp.where(lane >= COLS, label, 0.0), 64, axis=1)
    last = jnp.where(lane < 8, last, 0.0)
    first = pltpu.roll(jnp.where(lane < 16, label, 0.0), 64, axis=1)
    blank = jnp.zeros((ROWS, C - 128), F32)

    def wide(part):
        return jnp.concatenate([part, blank], axis=-1).astype(BF16)

    own_lab[...] = label.astype(BF16)
    to_next[0:area, :] = tokens[9:16].reshape(area, C)
    to_next[area : area + ROWS, :] = wide(label)
    to_prev[0:area, :] = tokens[0:7].reshape(area, C)
    to_prev[area : area + ROWS, :] = wide(label)
    to_right[0:128, :] = (
        tokens[:, 48:64, :].astype(F32)[:, 8:16, :].reshape(128, C).astype(BF16)
    )
    to_right[128:144, :] = wide(last)
    to_left[0:128, :] = tokens[:, 0:16, :].astype(F32)[:, 0:8, :].reshape(128, C).astype(BF16)
    to_left[128:144, :] = wide(first)


def pack(tokens, regions):
    vmem = pl.BlockSpec(memory_space=pltpu.VMEM)
    rows = 7 * COLS + ROWS
    shapes = ((rows, C), (rows, C), (144, C), (144, C), (ROWS, 128))
    return pl.pallas_call(
        pack_kernel,
        out_shape=tuple(jax.ShapeDtypeStruct(shape, BF16) for shape in shapes),
        in_specs=[vmem] * 2,
        out_specs=(vmem,) * 5,
        compiler_params=pltpu.CompilerParams(vmem_limit_bytes=16 * 1024 * 1024),
        cost_estimate=pl.CostEstimate(flops=0, bytes_accessed=4_000_000, transcendentals=0),
    )(tokens, regions)


def fine_level(offs, up, down, left, right, up_c, down_c, own_lab, own, gain, coarse_gain,
               w_qkv, w_proj, w_merge):
    vmem = pl.BlockSpec(memory_space=pltpu.VMEM)
    anywhere = pl.BlockSpec(memory_space=pltpu.HBM)
    return pl.pallas_call(
        fine_kernel,
        out_shape=(
            jax.ShapeDtypeStruct((ROWS, COLS, C), BF16),
            jax.ShapeDtypeStruct((256, CC), BF16),
            jax.ShapeDtypeStruct((128, CC), BF16),
            jax.ShapeDtypeStruct((128, CC), BF16),
        ),
        in_specs=[pl.BlockSpec(memory_space=pltpu.SMEM)] + [vmem] * 7 + [anywhere] * 6,
        out_specs=(vmem,) * 4,
        scratch_shapes=[
            pltpu.VMEM((32, 10, 8, C), F32),
            pltpu.VMEM((32, 128), F32),
            pltpu.VMEM((WINS * 64, C), BF16),
            pltpu.VMEM((WINS * 64, 3 * C), BF16),
            pltpu.VMEM((24, WINS, 8, C), F32),
            pltpu.VMEM((4, ROWS, COLS, 128), F32),
            pltpu.VMEM((256, 4 * C), BF16),
            pltpu.VMEM((ROWS, COLS, C), BF16),
            pltpu.VMEM((1, C), F32),
            pltpu.VMEM((1, CC), F32),
            pltpu.VMEM((C, 3 * C), BF16),
            pltpu.VMEM((C, C), BF16),
            pltpu.VMEM((4 * C, CC), BF16),
            pltpu.SemaphoreType.DMA((6,)),
        ],
        compiler_params=pltpu.CompilerParams(vmem_limit_bytes=MOST),
        cost_estimate=pl.CostEstimate(
            flops=9_000_000_000, bytes_accessed=12_000_000, transcendentals=1_000_000
        ),
    )(offs, up, down, left, right, up_c, down_c, own_lab, own, gain, coarse_gain,
      w_qkv, w_proj, w_merge)


def coarse_kernel(x_a, x_b, weights, out_a, out_b, x, hidden):
    shards, _, depth, width = weights.shape
    half = x_a.shape[0]
    x[0:half, :] = x_a[...]
    x[half : 2 * half, :] = x_b[...]
    for n in range(width // 256):
        cols = slice(256 * n, 256 * n + 256)
        before = dot(x[...], weights[:, 0, :, cols].reshape(CC, 256))
        hidden[:, cols] = (
            0.5 * before * (1.0 + lax.erf(before * np.float32(np.sqrt(0.5))))
        ).astype(BF16)
    for n in range(CC // 256):
        cols = slice(256 * n, 256 * n + 256)
        span = weights[256 // depth * n : 256 // depth * (n + 1), 1].reshape(256, width)
        value = dot(hidden[...], span, ((1,), (1,))).astype(out_a.dtype)
        out_a[:, cols] = value[:half]
        out_b[:, cols] = value[half:]


def coarse_level(x_a, x_b, weights, dtype):
    width = weights.shape[-1]
    rows = x_a.shape[0]
    vmem = pl.BlockSpec(memory_space=pltpu.VMEM)
    return pl.pallas_call(
        coarse_kernel,
        out_shape=(jax.ShapeDtypeStruct(x_a.shape, dtype),) * 2,
        in_specs=[vmem] * 3,
        out_specs=(vmem, vmem),
        scratch_shapes=[
            pltpu.VMEM((2 * rows, CC), BF16),
            pltpu.VMEM((2 * rows, width), BF16),
        ],
        compiler_params=pltpu.CompilerParams(vmem_limit_bytes=40 * 1024 * 1024),
        cost_estimate=pl.CostEstimate(
            flops=8 * rows * CC * width, bytes_accessed=10_000_000, transcendentals=0
        ),
    )(x_a, x_b, weights)


def ring(count, step):
    return [(i, (i + step) % count) for i in range(count)]


def on_device(
    tokens, offsets, regions, norm_gain, w_qkv, w_proj, w_merge, coarse_gain, w_in, w_out
):
    rows_axes, rows_n = ("lat", "inner"), lax.axis_size(("lat", "inner"))
    cols_axes, cols_n = ("y", "x", "core"), lax.axis_size(("y", "x", "core"))
    weights = lax.all_gather(jnp.stack([w_in, w_out.T]), cols_axes, axis=0, tiled=False)
    to_next, to_prev, to_right, to_left, own_lab = pack(tokens, regions)
    up = lax.ppermute(to_next, rows_axes, ring(rows_n, 1))
    down = lax.ppermute(to_prev, rows_axes, ring(rows_n, -1))
    left = lax.ppermute(to_right, cols_axes, ring(cols_n, 1))
    right = lax.ppermute(to_left, cols_axes, ring(cols_n, -1))
    side_lab = left[128:] + right[128:]
    up_c = lax.ppermute(
        jnp.concatenate([left[72:128], right[72:128], side_lab]), rows_axes, ring(rows_n, 1)
    )
    down_c = lax.ppermute(
        jnp.concatenate([left[:56], right[:56], side_lab]), rows_axes, ring(rows_n, -1)
    )
    fine_out, coarse, normed_a, normed_b = fine_level(
        offsets, up, down, left, right, up_c, down_c, own_lab, tokens,
        norm_gain.reshape(1, -1), coarse_gain.reshape(1, -1), w_qkv, w_proj, w_merge,
    )
    their_a = lax.ppermute(normed_a, rows_axes, ring(rows_n, 1))
    their_b = lax.ppermute(normed_b, rows_axes, ring(rows_n, -1))
    part_a, part_b = coarse_level(their_a, their_b, weights, BF16)
    back_a = lax.ppermute(part_a, rows_axes, ring(rows_n, -1))
    back_b = lax.ppermute(part_b, rows_axes, ring(rows_n, 1))
    own_a, own_b = coarse_level(normed_a, normed_b, weights, F32)
    change = jnp.concatenate([own_a + back_a.astype(F32), own_b + back_b.astype(F32)])
    coarse_out = (coarse.astype(F32) + change).astype(BF16)
    return fine_out, coarse_out.reshape(ROWS // 2, COLS // 2, CC)


def solution(mesh):
    fine_mesh = Mesh(
        np.array(mesh.devices).reshape(4, 4, 4, 2, 2), ("lat", "y", "x", "core", "inner")
    )
    lon = ("y", "x", "core")
    placed = (
        P(("lat", "inner"), lon, None),
        P(),
        P(("lat", "inner"), lon),
        P(),
        P(),
        P(),
        P(),
        P(),
        P(lon, "inner"),
        P("inner", lon),
    )
    return jax.shard_map(
        on_device,
        mesh=fine_mesh,
        in_specs=placed,
        out_specs=(P(("lat", "inner"), lon, None), P(("lat", "inner"), lon, None)),
        check_vma=False,
    )
```

time: 119 us -> 98.6 us (0.83)
  the two profiles are of different devices: /device:TPU:6 before, /device:TPU:1 now
where the time goes in v2:
time: 98.6 us; the launch traced here: 98.4 us
  waiting for transfers between devices  30.9 us (31%)
  Pallas kernels  24.9 us (25%)
  starting transfers between devices  19.2 us (19%)
  between operations  14.2 us (14%)
  local copies, waits for them, and re-layouts  6.36 us (6%)
  other arithmetic  2.78 us (3%)
    pallas_call x1, Pallas kernels, fine_level(): pl.pallas_call(fine_kernel, out_shape=(jax.ShapeDtypeStruct((ROWS, COLS,...  19.9 us
    all_gather x1, waiting for transfers between devices, on_device(): lax.all_gather(jnp.stack([w_in, w_out.T]), cols_axes, axis=0, tiled=False)  13.7 us
    unnamed x28, local copies, waits for them, and re-layouts  6.34 us
    ppermute x1, starting transfers between devices, on_device(): lax.ppermute(jnp.concatenate([left[:56], right[:56], side_lab]), rows_axe...  4.89 us
    pallas_call x2, Pallas kernels, coarse_level(): pl.pallas_call(coarse_kernel, out_shape=(jax.ShapeDtypeStruct(x_a.shape,...  4.86 us
    ppermute x1, waiting for transfers between devices, on_device(): their_a = lax.ppermute(normed_a, rows_axes, ring(rows_n, 1))  4.37 us
    ppermute x1, waiting for transfers between devices, on_device(): lax.ppermute(jnp.concatenate([left[:56], right[:56], side_lab]), rows_axe...  4.01 us
    ppermute x1, starting transfers between devices, on_device(): down = lax.ppermute(to_prev, rows_axes, ring(rows_n, -1))  3.94 us
  transfers between devices with their start and end apart: 11, of which 6 were waited for; matrix products, arithmetic and copies ran while one was open for 0% of the time, Pallas kernels for 23%

profile of v2, /device:TPU:1, one launch (start us, length us, event | category | flops | bytes accessed | tf_op | source)
XLA Modules:
  0.0 98.4 jit_solution(5594838614710228406)
XLA Ops:
  7.2 0.0 all-gather.3.cloned.1.call-start
  7.2 1.7 %pad_maximum_fusion = bf16[2,32,2048]{2,1,0:T(8,128)(2,1)} fusion(bf16[1,32,2048]{2,1,0:T(8,128)(2,1)} %bitcast.11, bf16[1,32,2048]{2,1,0:T(8,128)(2,1)} %bitcast.12), kind=kLoop, calls=%fused_computation.4 | loop fusion | flops 131072 | bytes 524288 | tf_op jit(solution)/shard_map/stack | solution.py:337
  8.9 0.0 all-gather.3.cloned.1.call-update
  8.9 0.0 copy-start.2
  8.9 1.2 %copy-done.2 = bf16[16,64,512]{2,1,0:T(8,128)(2,1)S(1)} copy-done((bf16[16,64,512]{2,1,0:T(8,128)(2,1)S(1)}, bf16[16,64,512]{2,1,0:T(8,128)(2,1)}, u32[]{:S(2)}) %copy-start.2) | copy-done | bytes 1048600
  10.2 0.0 copy-start.5
  10.2 0.7 copy-done.5
  10.9 0.1 shard_map.113
  11.0 0.0 copy-start.6
  11.0 2.6 %collective-permute-start.2 = (bf16[144,512]{1,0:T(8,128)(2,1)S(1)}, bf16[144,512]{1,0:T(8,128)(2,1)S(1)}, u32[]{:S(2)}, u32[]{:S(2)}) collective-permute-start(bf16[144,512]{1,0:T(8,128)(2,1)S(1)} %get-tuple-element.17), channel_id=1, source_target_pairs={{0,2},{2,4},{4,6},{6,8},{8,10},{10,12},{12,14},{14,16},{16,18},{18... | collective-permute-start | bytes 442376 | tf_op jit(solution)/shard_map/ppermute | solution.py:341
  13.6 0.7 collective-permute-start.3
  14.4 0.9 collective-permute-start
  15.3 3.9 %collective-permute-start.1 = (bf16[464,512]{1,0:T(8,128)(2,1)S(1)}, bf16[464,512]{1,0:T(8,128)(2,1)S(1)}, u32[]{:S(2)}, u32[]{:S(2)}) collective-permute-start(bf16[464,512]{1,0:T(8,128)(2,1)S(1)} %get-tuple-element.16), channel_id=1, source_target_pairs={{0,193},{1,0},{64,1},{65,64},{128,65},{129,128},{192,129},{193,192... | collective-permute-start | bytes 1425416 | tf_op jit(solution)/shard_map/ppermute | solution.py:340
  19.2 0.0 collective-permute-done.2.left
  19.2 0.0 copy-start.8
  19.2 0.0 collective-permute-done.3.right
  19.2 0.0 copy-start.9
  19.3 4.9 %collective-permute-start.5 = (bf16[128,512]{1,0:T(8,128)(2,1)S(1)}, bf16[128,512]{1,0:T(8,128)(2,1)S(1)}, u32[]{:S(2)}, u32[]{:S(2)}) collective-permute-start(bf16[128,512]{1,0:T(8,128)(2,1)S(1)} %get-tuple-element.32), channel_id=1, source_target_pairs={{0,193},{1,0},{64,1},{65,64},{128,65},{129,128},{192,129},{193,192... | collective-permute-start | bytes 393224 | tf_op jit(solution)/shard_map/ppermute | solution.py:347
  24.2 0.0 collective-permute-start.4
  24.2 4.0 %collective-permute-done.5.down_c = bf16[128,512]{1,0:T(8,128)(2,1)S(1)} collective-permute-done((bf16[128,512]{1,0:T(8,128)(2,1)S(1)}, bf16[128,512]{1,0:T(8,128)(2,1)S(1)}, u32[]{:S(2)}, u32[]{:S(2)}) %collective-permute-start.5) | collective-permute-done | bytes 131104 | tf_op jit(solution)/shard_map/ppermute | solution.py:347
  28.2 0.0 copy-start.12
  28.2 2.8 %collective-permute-done.4.up_c = bf16[128,512]{1,0:T(8,128)(2,1)S(1)} collective-permute-done((bf16[128,512]{1,0:T(8,128)(2,1)S(1)}, bf16[128,512]{1,0:T(8,128)(2,1)S(1)}, u32[]{:S(2)}, u32[]{:S(2)}) %collective-permute-start.4) | collective-permute-done | bytes 131104 | tf_op jit(solution)/shard_map/ppermute | solution.py:344
  31.0 0.0 copy-start.13
  31.0 0.0 collective-permute-done.up
  31.0 0.0 copy-start.10
  31.0 0.0 collective-permute-done.1.down
  31.0 0.0 copy-done.6
  31.0 0.0 copy-start.11
  31.0 0.0 copy-done.8
  31.0 0.0 copy-done.9
  31.1 0.0 copy-done.12
  31.1 0.6 copy-done.13
  31.6 0.3 copy-done.10
  31.9 0.2 copy-done.11
  32.1 19.9 %shard_map.114 = (bf16[16,64,512]{2,1,0:T(8,128)(2,1)}, bf16[256,1024]{1,0:T(8,128)(2,1)}, bf16[128,1024]{1,0:T(8,128)(2,1)}, bf16[128,1024]{1,0:T(8,128)(2,1)}) custom-call(s32[2]{0:T(128)} %offs.1, bf16[464,512]{1,0:T(8,128)(2,1)} %copy-done.10, bf16[464,512]{1,0:T(8,128)(2,1)} %copy-done.11, bf16[144,512]{1,0:T(8,128)(2,1)} %copy-done.8, ...), custom_call_target="tpu_custom_call" | custom-call | flops 8999999488 | bytes 12000000 | tf_op jit(solution)/shard_map/pallas_call | solution.py:255
  52.0 0.1 collective-permute-start.6
  52.1 2.7 %collective-permute-start.7 = (bf16[128,1024]{1,0:T(8,128)(2,1)}, bf16[128,1024]{1,0:T(8,128)(2,1)S(1)}, u32[]{:S(2)}, u32[]{:S(2)}) collective-permute-start(bf16[128,1024]{1,0:T(8,128)(2,1)} %get-tuple-element.23.x_b), channel_id=1, source_target_pairs={{0,193},{1,0},{64,1},{65,64},{128,65},{129,128},{192,129},{193,192... | collective-permute-start | bytes 786440 | tf_op jit(solution)/shard_map/ppermute | solution.py:355
  54.7 4.4 %collective-permute-done.6.x_a = bf16[128,1024]{1,0:T(8,128)(2,1)S(1)} collective-permute-done((bf16[128,1024]{1,0:T(8,128)(2,1)}, bf16[128,1024]{1,0:T(8,128)(2,1)S(1)}, u32[]{:S(2)}, u32[]{:S(2)}) %collective-permute-start.6) | collective-permute-done | bytes 262176 | tf_op jit(solution)/shard_map/ppermute | solution.py:354
  59.1 0.0 collective-permute-done.7.x_b
  59.1 13.7 %all-gather.3.cloned.1.call-done = bf16[64,32,2048]{2,1,0:T(8,128)(2,1)} async-done(((bf16[2,32,2048]{2,1,0:T(8,128)(2,1)}), bf16[64,32,2048]{2,1,0:T(8,128)(2,1)}) %all-gather.3.cloned.1.call-update) | async-done | bytes 8388624 | tf_op jit(solution)/shard_map/all_gather | solution.py:337
  72.8 0.0 copy-start
  72.8 3.4 %copy-done = bf16[64,32,2048]{2,1,0:T(8,128)(2,1)S(1)} copy-done((bf16[64,32,2048]{2,1,0:T(8,128)(2,1)S(1)}, bf16[64,32,2048]{2,1,0:T(8,128)(2,1)}, u32[]{:S(2)}) %copy-start) | copy-done | bytes 8388632
  76.2 0.0 copy-start.1
  76.2 0.0 copy-start.3
  76.2 0.0 copy-start.4
  76.2 2.4 %shard_map.116 = (bf16[128,1024]{1,0:T(8,128)(2,1)S(1)}, bf16[128,1024]{1,0:T(8,128)(2,1)S(1)}) custom-call(bf16[128,1024]{1,0:T(8,128)(2,1)S(1)} %collective-permute-done.6.x_a, bf16[128,1024]{1,0:T(8,128)(2,1)S(1)} %collective-permute-done.7.x_b, bf16[32,2,32,2048]{3,2,1,0:T(8,128)(2,1)S(1)} %bitcast.8), custom_call_target="tpu_custom_call" | custom-call | flops 2147483648 | bytes 10000000 | tf_op jit(solution)/shard_map/pallas_call | solution.py:312
  78.6 3.3 %collective-permute-start.8 = (bf16[128,1024]{1,0:T(8,128)(2,1)S(1)}, bf16[128,1024]{1,0:T(8,128)(2,1)S(1)}, u32[]{:S(2)}, u32[]{:S(2)}) collective-permute-start(bf16[128,1024]{1,0:T(8,128)(2,1)S(1)} %get-tuple-element.25), channel_id=1, source_target_pairs={{0,193},{1,0},{64,1},{65,64},{128,65},{129,128},{192,129},{193,192... | collective-permute-start | bytes 786440 | tf_op jit(solution)/shard_map/ppermute | solution.py:357
  81.9 0.0 copy-start.7
  81.9 0.0 collective-permute-start.9
  81.9 0.0 copy-done.1
  81.9 0.0 copy-done.3
  82.0 0.0 copy-done.4
  82.0 2.4 %shard_map.115 = (f32[128,1024]{1,0:T(8,128)S(1)}, f32[128,1024]{1,0:T(8,128)S(1)}) custom-call(bf16[128,1024]{1,0:T(8,128)(2,1)S(1)} %copy-done.3, bf16[128,1024]{1,0:T(8,128)(2,1)S(1)} %copy-done.4, bf16[32,2,32,2048]{3,2,1,0:T(8,128)(2,1)S(1)} %bitcast.9), custom_call_target="tpu_custom_call" | custom-call | flops 2147483648 | bytes 10000000 | tf_op jit(solution)/shard_map/pallas_call | solution.py:312
  84.4 3.0 %collective-permute-done.8 = bf16[128,1024]{1,0:T(8,128)(2,1)S(1)} collective-permute-done((bf16[128,1024]{1,0:T(8,128)(2,1)S(1)}, bf16[128,1024]{1,0:T(8,128)(2,1)S(1)}, u32[]{:S(2)}, u32[]{:S(2)}) %collective-permute-start.8) | collective-permute-done | bytes 262176 | tf_op jit(solution)/shard_map/ppermute | solution.py:357
  87.4 0.1 convert_add_fusion.1
  87.5 3.0 %collective-permute-done.9 = bf16[128,1024]{1,0:T(8,128)(2,1)S(1)} collective-permute-done((bf16[128,1024]{1,0:T(8,128)(2,1)S(1)}, bf16[128,1024]{1,0:T(8,128)(2,1)S(1)}, u32[]{:S(2)}, u32[]{:S(2)}) %collective-permute-start.9) | collective-permute-done | bytes 262176 | tf_op jit(solution)/shard_map/ppermute | solution.py:358
  90.5 0.1 convert_add_fusion
  90.6 0.0 copy-done.7
  90.6 0.9 fusion
  (4 shorter events, 0.1 us)
Async XLA Ops:
  7.2 65.6 %all-gather.3.cloned.1.call-start = ((), (), s32[]{:S(2)}) async-start(), calls=%async_computation | async-start | bytes 8650752 | tf_op jit(solution)/shard_map/all_gather | solution.py:337
  8.9 1.2 %copy-start.2 = (bf16[16,64,512]{2,1,0:T(8,128)(2,1)S(1)}, bf16[16,64,512]{2,1,0:T(8,128)(2,1)}, u32[]{:S(2)}) copy-start(bf16[16,64,512]{2,1,0:T(8,128)(2,1)} %own_hbm.1) | copy-start | bytes 3145732
  10.2 0.7 copy-start.5
  11.0 20.0 %copy-start.6 = (bf16[16,128]{1,0:T(8,128)(2,1)}, bf16[16,128]{1,0:T(8,128)(2,1)S(1)}, u32[]{:S(2)}) copy-start(bf16[16,128]{1,0:T(8,128)(2,1)S(1)} %get-tuple-element.19.own_lab) | copy-start | bytes 12292
  11.0 8.2 %collective-permute-start.2 = (bf16[144,512]{1,0:T(8,128)(2,1)S(1)}, bf16[144,512]{1,0:T(8,128)(2,1)S(1)}, u32[]{:S(2)}, u32[]{:S(2)}) collective-permute-start(bf16[144,512]{1,0:T(8,128)(2,1)S(1)} %get-tuple-element.17), channel_id=1, source_target_pairs={{0,2},{2,4},{4,6},{6,8},{8,10},{10,12},{12,14},{14,16},{16,18},{18... | collective-permute-start | bytes 442376 | tf_op jit(solution)/shard_map/ppermute | solution.py:341
  13.6 5.6 %collective-permute-start.3 = (bf16[144,512]{1,0:T(8,128)(2,1)S(1)}, bf16[144,512]{1,0:T(8,128)(2,1)S(1)}, u32[]{:S(2)}, u32[]{:S(2)}) collective-permute-start(bf16[144,512]{1,0:T(8,128)(2,1)S(1)} %get-tuple-element.18), channel_id=1, source_target_pairs={{0,62},{2,0},{4,2},{6,4},{8,6},{10,8},{12,10},{14,12},{16,14},{18,... | collective-permute-start | bytes 442376 | tf_op jit(solution)/shard_map/ppermute | solution.py:342
  14.4 16.6 %collective-permute-start = (bf16[464,512]{1,0:T(8,128)(2,1)S(1)}, bf16[464,512]{1,0:T(8,128)(2,1)S(1)}, u32[]{:S(2)}, u32[]{:S(2)}) collective-permute-start(bf16[464,512]{1,0:T(8,128)(2,1)S(1)} %get-tuple-element.15), channel_id=1, source_target_pairs={{0,1},{1,64},{64,65},{65,128},{128,129},{129,192},{192,193},{193,0... | collective-permute-start | bytes 1425416 | tf_op jit(solution)/shard_map/ppermute | solution.py:339
  15.3 15.7 %collective-permute-start.1 = (bf16[464,512]{1,0:T(8,128)(2,1)S(1)}, bf16[464,512]{1,0:T(8,128)(2,1)S(1)}, u32[]{:S(2)}, u32[]{:S(2)}) collective-permute-start(bf16[464,512]{1,0:T(8,128)(2,1)S(1)} %get-tuple-element.16), channel_id=1, source_target_pairs={{0,193},{1,0},{64,1},{65,64},{128,65},{129,128},{192,129},{193,192... | collective-permute-start | bytes 1425416 | tf_op jit(solution)/shard_map/ppermute | solution.py:340
  19.2 11.8 %copy-start.8 = (bf16[144,512]{1,0:T(8,128)(2,1)}, bf16[144,512]{1,0:T(8,128)(2,1)S(1)}, u32[]{:S(2)}) copy-start(bf16[144,512]{1,0:T(8,128)(2,1)S(1)} %collective-permute-done.2.left) | copy-start | bytes 442372
  19.2 11.8 %copy-start.9 = (bf16[144,512]{1,0:T(8,128)(2,1)}, bf16[144,512]{1,0:T(8,128)(2,1)S(1)}, u32[]{:S(2)}) copy-start(bf16[144,512]{1,0:T(8,128)(2,1)S(1)} %collective-permute-done.3.right) | copy-start | bytes 442372
  19.3 8.9 %collective-permute-start.5 = (bf16[128,512]{1,0:T(8,128)(2,1)S(1)}, bf16[128,512]{1,0:T(8,128)(2,1)S(1)}, u32[]{:S(2)}, u32[]{:S(2)}) collective-permute-start(bf16[128,512]{1,0:T(8,128)(2,1)S(1)} %get-tuple-element.32), channel_id=1, source_target_pairs={{0,193},{1,0},{64,1},{65,64},{128,65},{129,128},{192,129},{193,192... | collective-permute-start | bytes 393224 | tf_op jit(solution)/shard_map/ppermute | solution.py:347
  24.2 6.8 %collective-permute-start.4 = (bf16[128,512]{1,0:T(8,128)(2,1)S(1)}, bf16[128,512]{1,0:T(8,128)(2,1)S(1)}, u32[]{:S(2)}, u32[]{:S(2)}) collective-permute-start(bf16[128,512]{1,0:T(8,128)(2,1)S(1)} %get-tuple-element.33), channel_id=1, source_target_pairs={{0,1},{1,64},{64,65},{65,128},{128,129},{129,192},{192,193},{193,0... | collective-permute-start | bytes 393224 | tf_op jit(solution)/shard_map/ppermute | solution.py:344
  28.2 2.8 %copy-start.12 = (bf16[128,512]{1,0:T(8,128)(2,1)}, bf16[128,512]{1,0:T(8,128)(2,1)S(1)}, u32[]{:S(2)}) copy-start(bf16[128,512]{1,0:T(8,128)(2,1)S(1)} %collective-permute-done.5.down_c) | copy-start | bytes 393220
  31.0 0.6 copy-start.13
  31.0 0.9 copy-start.10
  31.0 1.0 %copy-start.11 = (bf16[464,512]{1,0:T(8,128)(2,1)}, bf16[464,512]{1,0:T(8,128)(2,1)S(1)}, u32[]{:S(2)}) copy-start(bf16[464,512]{1,0:T(8,128)(2,1)S(1)} %collective-permute-done.1.down) | copy-start | bytes 1425412
  52.0 7.1 %collective-permute-start.6 = (bf16[128,1024]{1,0:T(8,128)(2,1)}, bf16[128,1024]{1,0:T(8,128)(2,1)S(1)}, u32[]{:S(2)}, u32[]{:S(2)}) collective-permute-start(bf16[128,1024]{1,0:T(8,128)(2,1)} %get-tuple-element.22.x_a), channel_id=1, source_target_pairs={{0,1},{1,64},{64,65},{65,128},{128,129},{129,192},{192,193},{193,0... | collective-permute-start | bytes 786440 | tf_op jit(solution)/shard_map/ppermute | solution.py:354
  52.1 7.0 %collective-permute-start.7 = (bf16[128,1024]{1,0:T(8,128)(2,1)}, bf16[128,1024]{1,0:T(8,128)(2,1)S(1)}, u32[]{:S(2)}, u32[]{:S(2)}) collective-permute-start(bf16[128,1024]{1,0:T(8,128)(2,1)} %get-tuple-element.23.x_b), channel_id=1, source_target_pairs={{0,193},{1,0},{64,1},{65,64},{128,65},{129,128},{192,129},{193,192... | collective-permute-start | bytes 786440 | tf_op jit(solution)/shard_map/ppermute | solution.py:355
  72.8 3.4 %copy-start = (bf16[64,32,2048]{2,1,0:T(8,128)(2,1)S(1)}, bf16[64,32,2048]{2,1,0:T(8,128)(2,1)}, u32[]{:S(2)}) copy-start(bf16[64,32,2048]{2,1,0:T(8,128)(2,1)} %all-gather.3.cloned.1.call-done) | copy-start | bytes 25165828
  76.2 5.8 %copy-start.1 = (bf16[64,32,2048]{2,1,0:T(8,128)(2,1)S(1)}, bf16[64,32,2048]{2,1,0:T(8,128)(2,1)}, u32[]{:S(2)}) copy-start(bf16[64,32,2048]{2,1,0:T(8,128)(2,1)} %all-gather.3.cloned.1.call-done) | copy-start | bytes 25165828
  76.2 5.8 %copy-start.3 = (bf16[128,1024]{1,0:T(8,128)(2,1)S(1)}, bf16[128,1024]{1,0:T(8,128)(2,1)}, u32[]{:S(2)}) copy-start(bf16[128,1024]{1,0:T(8,128)(2,1)} %get-tuple-element.22.x_a) | copy-start | bytes 786436
  76.2 5.8 %copy-start.4 = (bf16[128,1024]{1,0:T(8,128)(2,1)S(1)}, bf16[128,1024]{1,0:T(8,128)(2,1)}, u32[]{:S(2)}) copy-start(bf16[128,1024]{1,0:T(8,128)(2,1)} %get-tuple-element.23.x_b) | copy-start | bytes 786436
  78.6 8.8 %collective-permute-start.8 = (bf16[128,1024]{1,0:T(8,128)(2,1)S(1)}, bf16[128,1024]{1,0:T(8,128)(2,1)S(1)}, u32[]{:S(2)}, u32[]{:S(2)}) collective-permute-start(bf16[128,1024]{1,0:T(8,128)(2,1)S(1)} %get-tuple-element.25), channel_id=1, source_target_pairs={{0,193},{1,0},{64,1},{65,64},{128,65},{129,128},{192,129},{193,192... | collective-permute-start | bytes 786440 | tf_op jit(solution)/shard_map/ppermute | solution.py:357
  81.9 8.6 %copy-start.7 = (bf16[256,1024]{1,0:T(8,128)(2,1)S(1)}, bf16[256,1024]{1,0:T(8,128)(2,1)}, u32[]{:S(2)}) copy-start(bf16[256,1024]{1,0:T(8,128)(2,1)} %get-tuple-element.21) | copy-start | bytes 1572868
  81.9 8.5 %collective-permute-start.9 = (bf16[128,1024]{1,0:T(8,128)(2,1)S(1)}, bf16[128,1024]{1,0:T(8,128)(2,1)S(1)}, u32[]{:S(2)}, u32[]{:S(2)}) collective-permute-start(bf16[128,1024]{1,0:T(8,128)(2,1)S(1)} %get-tuple-element.27), channel_id=1, source_target_pairs={{0,1},{1,64},{64,65},{65,128},{128,129},{129,192},{192,193},{193,0... | collective-permute-start | bytes 786440 | tf_op jit(solution)/shard_map/ppermute | solution.py:358
Sparse Core Ops, SparseCore 0:
  10.6 62.1 all-gather.2

commit v3 on v2

--- a/solution.py
+++ b/solution.py
@@ -17,6 +17,7 @@
 GROUP = 3
 QUAD = 256
 MOST = 62 * 1024 * 1024
+COARSE_LIMIT = 32 * 1024 * 1024
 F32 = jnp.float32
 BF16 = jnp.bfloat16
 
@@ -286,47 +287,83 @@
       w_qkv, w_proj, w_merge)
 
 
-def coarse_kernel(x_a, x_b, weights, out_a, out_b, x, hidden):
-    shards, _, depth, width = weights.shape
+def coarse_kernel(place, x_a, x_b, *rest):
+    own, other, (out_a, out_b, x, hidden) = rest[:4], rest[4:8], rest[8:]
     half = x_a.shape[0]
-    x[0:half, :] = x_a[...]
-    x[half : 2 * half, :] = x_b[...]
-    for n in range(width // 256):
-        cols = slice(256 * n, 256 * n + 256)
-        before = dot(x[...], weights[:, 0, :, cols].reshape(CC, 256))
-        hidden[:, cols] = (
-            0.5 * before * (1.0 + lax.erf(before * np.float32(np.sqrt(0.5))))
-        ).astype(BF16)
-    for n in range(CC // 256):
-        cols = slice(256 * n, 256 * n + 256)
-        span = weights[256 // depth * n : 256 // depth * (n + 1), 1].reshape(256, width)
-        value = dot(hidden[...], span, ((1,), (1,))).astype(out_a.dtype)
-        out_a[:, cols] = value[:half]
-        out_b[:, cols] = value[half:]
-
-
-def coarse_level(x_a, x_b, weights, dtype):
-    width = weights.shape[-1]
+    width = hidden.shape[-1]
+    slot_x = [(x_at + 4 - place[0]) % 4 for x_at in range(4)]
+    slot_y = [(y_at + 4 - place[1]) % 4 for y_at in range(4)]
+    for j in range(4):
+        at = pl.ds(pl.multiple_of((place[1] + j) % 4 * 256, 256), 256)
+        x[0:half, 256 * j : 256 * j + 256] = x_a[:, at]
+        x[half : 2 * half, 256 * j : 256 * j + 256] = x_b[:, at]
+
+    def work(w_in, w_out):
+        for n in range(width // 256):
+            cols = slice(256 * n, 256 * n + 256)
+            block = jnp.concatenate(
+                [w_in[i // 8][slot_x[i // 2 % 4], i % 2, :, cols] for i in range(32)], axis=0
+            )
+            before = dot(x[...], block)
+            hidden[:, cols] = (
+                0.5 * before * (1.0 + lax.erf(before * np.float32(np.sqrt(0.5))))
+            ).astype(BF16)
+        for n in range(4):
+            cols = slice(256 * n, 256 * n + 256)
+            span = jnp.concatenate(
+                [w_out[i // 2][slot_y[n], 1 - i % 2] for i in range(8)], axis=0
+            )
+            value = dot(hidden[...], span, ((1,), (1,)))
+            value = pltpu.roll(value, 64 * place[0], axis=1).astype(out_a.dtype)
+            out_a[:, cols] = value[:half]
+            out_b[:, cols] = value[half:]
+
+    @pl.when(place[2] == 0)
+    def _():
+        work(own, other)
+
+    @pl.when(place[2] == 1)
+    def _():
+        work(other, own)
+
+
+def coarse_level(place, x_a, x_b, pieces, dtype):
+    width = pieces[0].shape[-1]
     rows = x_a.shape[0]
     vmem = pl.BlockSpec(memory_space=pltpu.VMEM)
     return pl.pallas_call(
         coarse_kernel,
         out_shape=(jax.ShapeDtypeStruct(x_a.shape, dtype),) * 2,
-        in_specs=[vmem] * 3,
+        in_specs=[pl.BlockSpec(memory_space=pltpu.SMEM)] + [vmem] * 10,
         out_specs=(vmem, vmem),
         scratch_shapes=[
             pltpu.VMEM((2 * rows, CC), BF16),
             pltpu.VMEM((2 * rows, width), BF16),
         ],
-        compiler_params=pltpu.CompilerParams(vmem_limit_bytes=40 * 1024 * 1024),
+        compiler_params=pltpu.CompilerParams(vmem_limit_bytes=COARSE_LIMIT),
         cost_estimate=pl.CostEstimate(
             flops=8 * rows * CC * width, bytes_accessed=10_000_000, transcendentals=0
         ),
-    )(x_a, x_b, weights)
+    )(place, x_a, x_b, *pieces)
 
 
 def ring(count, step):
     return [(i, (i + step) % count) for i in range(count)]
+
+
+def from_ahead(block, steps, second):
+    pairs = []
+    for y in range(4):
+        for x in range(4):
+            for core in range(2):
+                on_x = (core == 0) != second
+                source = (y, (x + steps) % 4) if on_x else ((y + steps) % 4, x)
+                pairs.append(((source[0] * 4 + source[1]) * 2 + core, (y * 4 + x) * 2 + core))
+    return lax.ppermute(block, ("y", "x", "core"), pairs)
+
+
+def around(block, second):
+    return [block] + [from_ahead(block, steps, second) for steps in (1, 3, 2)]
 
 
 def on_device(
@@ -334,12 +371,18 @@
 ):
     rows_axes, rows_n = ("lat", "inner"), lax.axis_size(("lat", "inner"))
     cols_axes, cols_n = ("y", "x", "core"), lax.axis_size(("y", "x", "core"))
-    weights = lax.all_gather(jnp.stack([w_in, w_out.T]), cols_axes, axis=0, tiled=False)
+    core = lax.axis_index("core")
+    w_out = w_out.T
+    keep = jnp.where(core == 0, w_in, w_out)
+    give = jnp.where(core == 0, w_out, w_in)
+    pair = jnp.stack([keep, lax.ppermute(give, "core", ring(2, 1))])
     to_next, to_prev, to_right, to_left, own_lab = pack(tokens, regions)
     up = lax.ppermute(to_next, rows_axes, ring(rows_n, 1))
     down = lax.ppermute(to_prev, rows_axes, ring(rows_n, -1))
     left = lax.ppermute(to_right, cols_axes, ring(cols_n, 1))
     right = lax.ppermute(to_left, cols_axes, ring(cols_n, -1))
+    zero, one, three, two = around(pair, False)
+    strip = jnp.stack([zero, one, two, three])
     side_lab = left[128:] + right[128:]
     up_c = lax.ppermute(
         jnp.concatenate([left[72:128], right[72:128], side_lab]), rows_axes, ring(rows_n, 1)
@@ -347,16 +390,23 @@
     down_c = lax.ppermute(
         jnp.concatenate([left[:56], right[:56], side_lab]), rows_axes, ring(rows_n, -1)
     )
+    zero, one, three, two = around(strip, True)
+    far = [one, two, three]
+    last = lax.ppermute(strip, "core", ring(2, 1))
     fine_out, coarse, normed_a, normed_b = fine_level(
         offsets, up, down, left, right, up_c, down_c, own_lab, tokens,
         norm_gain.reshape(1, -1), coarse_gain.reshape(1, -1), w_qkv, w_proj, w_merge,
     )
+    far, last, normed_a, normed_b = lax.optimization_barrier((far, last, normed_a, normed_b))
+    swapped = [lax.ppermute(piece, "core", ring(2, 1)) for piece in far]
+    pieces = [strip] + far + [last] + swapped
     their_a = lax.ppermute(normed_a, rows_axes, ring(rows_n, 1))
     their_b = lax.ppermute(normed_b, rows_axes, ring(rows_n, -1))
-    part_a, part_b = coarse_level(their_a, their_b, weights, BF16)
+    place = jnp.stack([lax.axis_index("x"), lax.axis_index("y"), core])
+    part_a, part_b = coarse_level(place, their_a, their_b, pieces, BF16)
     back_a = lax.ppermute(part_a, rows_axes, ring(rows_n, -1))
     back_b = lax.ppermute(part_b, rows_axes, ring(rows_n, 1))
-    own_a, own_b = coarse_level(normed_a, normed_b, weights, F32)
+    own_a, own_b = coarse_level(place, normed_a, normed_b, pieces, F32)
     change = jnp.concatenate([own_a + back_a.astype(F32), own_b + back_b.astype(F32)])
     coarse_out = (coarse.astype(F32) + change).astype(BF16)
     return fine_out, coarse_out.reshape(ROWS // 2, COLS // 2, CC)

time: 98.6 us -> 86.6 us (0.88)
  waiting for transfers between devices: 30.9 us -> 14.3 us
  starting transfers between devices: 19.2 us -> 34.4 us
  between operations: 14.2 us -> 0.83 us
  Pallas kernels: 24.9 us -> 31.4 us
  local copies, waits for them, and re-layouts: 6.36 us -> 2.78 us
    ppermute x0 -> x11, starting transfers between devices: none -> 21.2 us  [the longest x6 7.88 us: from_ahead(): return lax.ppermute(block, ('y', 'x', 'core'), pairs)]
    all_gather x1 -> x0, waiting for transfers between devices: 13.7 us -> none  [on_device(): lax.all_gather(jnp.stack([w_in, w_out.T]), cols_axes, axis=0, tiled=False)]
    pallas_call x2, Pallas kernels: 4.86 us -> 11.3 us  [coarse_level(): pl.pallas_call(coarse_kernel, out_shape=(jax.ShapeDtypeStruct(x_a.shape,...]
    ppermute x0 -> x11, waiting for transfers between devices: none -> 5.85 us  [the longest x6 5.84 us: from_ahead(): return lax.ppermute(block, ('y', 'x', 'core'), pairs)]
    ppermute x1, waiting for transfers between devices: 4.01 us -> 0.01 us  [on_device(): lax.ppermute(jnp.concatenate([left[:56], right[:56], side_lab]), rows_axe...]
    unnamed x28 -> x24, local copies, waits for them, and re-layouts: 6.34 us -> 2.76 us
    ppermute x1, waiting for transfers between devices: 3 us -> 0.01 us  [on_device(): back_a = lax.ppermute(part_a, rows_axes, ring(rows_n, -1))]
    ppermute x1, waiting for transfers between devices: 2.77 us -> 0.01 us  [on_device(): lax.ppermute(jnp.concatenate([left[72:128], right[72:128], side_lab]), ro...]
  transfers between devices with their start and end apart: 11 -> 21, of which waited for: 6 -> 7; matrix products, arithmetic and copies ran while one was open for 0% -> 0% of each run, Pallas kernels for 23% -> 30%
where the time goes in v3:
time: 86.6 us; the launch traced here: 86 us
  starting transfers between devices  34.4 us (40%)
  Pallas kernels  31.4 us (36%)
  waiting for transfers between devices  14.3 us (17%)
  local copies, waits for them, and re-layouts  2.78 us (3%)
  other arithmetic  2.33 us (3%)
    pallas_call x1, Pallas kernels, fine_level(): pl.pallas_call(fine_kernel, out_shape=(jax.ShapeDtypeStruct((ROWS, COLS,...  19.9 us
    pallas_call x2, Pallas kernels, coarse_level(): pl.pallas_call(coarse_kernel, out_shape=(jax.ShapeDtypeStruct(x_a.shape,...  11.3 us
    ppermute x6, starting transfers between devices, from_ahead(): return lax.ppermute(block, ('y', 'x', 'core'), pairs)  7.88 us
    ppermute x1, waiting for transfers between devices, on_device(): their_a = lax.ppermute(normed_a, rows_axes, ring(rows_n, 1))  6.6 us
    ppermute x6, waiting for transfers between devices, from_ahead(): return lax.ppermute(block, ('y', 'x', 'core'), pairs)  5.84 us
    ppermute x3, starting transfers between devices, on_device(): swapped = [lax.ppermute(piece, 'core', ring(2, 1)) for piece in far]  5.14 us
    ppermute x1, starting transfers between devices, on_device(): last = lax.ppermute(strip, 'core', ring(2, 1))  4.82 us
    ppermute x1, starting transfers between devices, on_device(): down = lax.ppermute(to_prev, rows_axes, ring(rows_n, -1))  3.94 us
  transfers between devices with their start and end apart: 21, of which 7 were waited for; matrix products, arithmetic and copies ran while one was open for 0% of the time, Pallas kernels for 30%

profile of v3, /device:TPU:1, one launch (start us, length us, event | category | flops | bytes accessed | tf_op | source)
XLA Modules:
  0.0 86.0 jit_solution(15797893891892581201)
XLA Ops:
  0.6 1.0 %fusion.1 = (bf16[1,32,2048]{2,1,0:T(8,128)(2,1)S(1)}, bf16[32,2048]{1,0:T(8,128)(2,1)S(1)}) fusion(bf16[32,2048]{1,0:T(8,128)(2,1)} %param.18, bf16[2048,32]{0,1:T(8,128)(2,1)} %param.19, pred[]{:T(512)S(6)} %eq.4), kind=kLoop, calls=%fused_computation.10 | loop fusion | flops 131072 | bytes 524289 | tf_op jit(solution)/shard_map/stack | solution.py:378
  1.6 3.3 %collective-permute-start.6 = (bf16[32,2048]{1,0:T(8,128)(2,1)S(1)}, bf16[32,2048]{1,0:T(8,128)(2,1)S(1)}, u32[]{:S(2)}, u32[]{:S(2)}) collective-permute-start(bf16[32,2048]{1,0:T(8,128)(2,1)S(1)} %get-tuple-element.43), channel_id=1, source_target_pairs={{0,2},{2,0},{1,3},{3,1},{4,6},{6,4},{5,7},{7,5},{8,10},{10,8},{9,1... | collective-permute-start | bytes 393224 | tf_op jit(solution)/shard_map/ppermute | solution.py:378
  5.0 1.2 %copy-done = bf16[16,64,512]{2,1,0:T(8,128)(2,1)S(1)} copy-done((bf16[16,64,512]{2,1,0:T(8,128)(2,1)S(1)}, bf16[16,64,512]{2,1,0:T(8,128)(2,1)}, u32[]{:S(2)}) %copy-start) | copy-done | bytes 1048600
  6.2 0.7 copy-done.3
  6.9 0.1 shard_map.113
  7.0 0.0 collective-permute-start.2
  7.1 0.5 collective-permute-start.3
  7.6 0.5 collective-permute-start
  8.1 3.9 %collective-permute-start.1 = (bf16[464,512]{1,0:T(8,128)(2,1)S(1)}, bf16[464,512]{1,0:T(8,128)(2,1)S(1)}, u32[]{:S(2)}, u32[]{:S(2)}) collective-permute-start(bf16[464,512]{1,0:T(8,128)(2,1)S(1)} %get-tuple-element.22), channel_id=1, source_target_pairs={{0,193},{1,0},{64,1},{65,64},{128,65},{129,128},{192,129},{193,192... | collective-permute-start | bytes 1425416 | tf_op jit(solution)/shard_map/ppermute | solution.py:381
  12.0 0.0 collective-permute-done.6
  12.1 3.0 %collective-permute-start.8 = (bf16[2,32,2048]{2,1,0:T(8,128)(2,1)S(1)}, bf16[2,32,2048]{2,1,0:T(8,128)(2,1)S(1)}, u32[]{:S(2)}, u32[]{:S(2)}) collective-permute-start(bf16[2,32,2048]{2,1,0:T(8,128)(2,1)S(1)} %get-tuple-element.41), channel_id=1, source_target_pairs={{8,0},{34,2},{12,4},{38,6},{0,8},{42,10},{4,12},{46,14},{24,16},{5... | collective-permute-start | bytes 786440 | tf_op jit(solution)/shard_map/ppermute | solution.py:362
  15.1 0.0 collective-permute-done.2.left
  15.1 0.8 collective-permute-start.7
  15.9 0.0 collective-permute-done.3.right
  15.9 0.0 copy-start.7
  15.9 0.8 collective-permute-start.9
  16.7 2.2 %collective-permute-done.8 = bf16[2,32,2048]{2,1,0:T(8,128)(2,1)S(1)} collective-permute-done((bf16[2,32,2048]{2,1,0:T(8,128)(2,1)S(1)}, bf16[2,32,2048]{2,1,0:T(8,128)(2,1)S(1)}, u32[]{:S(2)}, u32[]{:S(2)}) %collective-permute-start.8) | collective-permute-done | bytes 262176 | tf_op jit(solution)/shard_map/ppermute | solution.py:362
  18.9 3.1 %collective-permute-start.5 = (bf16[128,512]{1,0:T(8,128)(2,1)S(1)}, bf16[128,512]{1,0:T(8,128)(2,1)S(1)}, u32[]{:S(2)}, u32[]{:S(2)}) collective-permute-start(bf16[128,512]{1,0:T(8,128)(2,1)S(1)} %get-tuple-element.48), channel_id=1, source_target_pairs={{0,193},{1,0},{64,1},{65,64},{128,65},{129,128},{192,129},{193,192... | collective-permute-start | bytes 393224 | tf_op jit(solution)/shard_map/ppermute | solution.py:390
  22.0 0.4 collective-permute-done.7
  22.4 0.0 collective-permute-start.4
  22.4 0.3 collective-permute-done.9
  22.7 0.1 pad_maximum_fusion.rest_0_
  22.8 4.8 %collective-permute-start.13 = (bf16[4,2,32,2048]{3,2,1,0:T(8,128)(2,1)S(1)}, bf16[4,2,32,2048]{3,2,1,0:T(8,128)(2,1)}, u32[]{:S(2)}, u32[]{:S(2)}) collective-permute-start(bf16[4,2,32,2048]{3,2,1,0:T(8,128)(2,1)S(1)} %pad_maximum_fusion.rest_0_), channel_id=1, source_target_pairs={{0,2},{2,0},{1,3},{3,1},{4,6},{6,4},{5,7},{7,5},{8,10},{10,8},{9,1... | collective-permute-start | bytes 3145736 | tf_op jit(solution)/shard_map/ppermute | solution.py:395
  27.6 0.0 collective-permute-done.5.down_c
  27.6 0.0 collective-permute-start.12
  27.6 0.0 collective-permute-done.4.up_c
  27.7 0.0 copy-start.11
  27.7 2.2 %collective-permute-start.11 = (bf16[4,2,32,2048]{3,2,1,0:T(8,128)(2,1)S(1)}, bf16[4,2,32,2048]{3,2,1,0:T(8,128)(2,1)}, u32[]{:S(2)}, u32[]{:S(2)}) collective-permute-start(bf16[4,2,32,2048]{3,2,1,0:T(8,128)(2,1)S(1)} %pad_maximum_fusion.rest_0_), channel_id=1, source_target_pairs={{32,0},{10,2},{36,4},{14,6},{40,8},{2,10},{44,12},{6,14},{48,16},{... | collective-permute-start | bytes 3145736 | tf_op jit(solution)/shard_map/ppermute | solution.py:362
  29.9 0.0 collective-permute-done.up
  29.9 1.2 %collective-permute-start.10 = (bf16[4,2,32,2048]{3,2,1,0:T(8,128)(2,1)S(1)}, bf16[4,2,32,2048]{3,2,1,0:T(8,128)(2,1)}, u32[]{:S(2)}, u32[]{:S(2)}) collective-permute-start(bf16[4,2,32,2048]{3,2,1,0:T(8,128)(2,1)S(1)} %pad_maximum_fusion.rest_0_), channel_id=1, source_target_pairs={{16,0},{6,2},{20,4},{10,6},{24,8},{14,10},{28,12},{2,14},{32,16},{... | collective-permute-start | bytes 3145736 | tf_op jit(solution)/shard_map/ppermute | solution.py:362
  31.0 0.0 collective-permute-done.1.down
  31.0 0.0 copy-done.4
  31.0 0.8 copy-done.9
  31.8 0.0 copy-done.11
  31.8 0.0 copy-done.6
  31.8 0.0 copy-done.10
  31.8 0.0 copy-done.8
  31.8 19.9 %shard_map.114 = (bf16[16,64,512]{2,1,0:T(8,128)(2,1)}, bf16[256,1024]{1,0:T(8,128)(2,1)}, bf16[128,1024]{1,0:T(8,128)(2,1)}, bf16[128,1024]{1,0:T(8,128)(2,1)}) custom-call(s32[2]{0:T(128)} %offs.1, bf16[464,512]{1,0:T(8,128)(2,1)} %copy-done.8, bf16[464,512]{1,0:T(8,128)(2,1)} %copy-done.9, bf16[144,512]{1,0:T(8,128)(2,1)} %copy-done.6, ...), custom_call_target="tpu_custom_call" | custom-call | flops 8999999488 | bytes 12000000 | tf_op jit(solution)/shard_map/pallas_call | solution.py:256
  51.8 0.0 collective-permute-done.13.rest_4_
  51.8 2.4 %collective-permute-done.12.rest_3_ = bf16[4,2,32,2048]{3,2,1,0:T(8,128)(2,1)} collective-permute-done((bf16[4,2,32,2048]{3,2,1,0:T(8,128)(2,1)S(1)}, bf16[4,2,32,2048]{3,2,1,0:T(8,128)(2,1)}, u32[]{:S(2)}, u32[]{:S(2)}) %collective-permute-start.12) | collective-permute-done | bytes 1048608 | tf_op jit(solution)/shard_map/ppermute | solution.py:362
  54.1 0.0 collective-permute-done.11.rest_2_
  54.1 0.6 collective-permute-done.10.rest_1_
  54.8 4.6 %collective-permute-start.14 = (bf16[4,2,32,2048]{3,2,1,0:T(8,128)(2,1)}, bf16[4,2,32,2048]{3,2,1,0:T(8,128)(2,1)S(1)}, u32[]{:S(2)}, u32[]{:S(2)}) collective-permute-start(bf16[4,2,32,2048]{3,2,1,0:T(8,128)(2,1)} %collective-permute-done.10.rest_1_), channel_id=1, source_target_pairs={{0,2},{2,0},{1,3},{3,1},{4,6},{6,4},{5,7},{7,5},{8,10},{10,8},{9,1... | collective-permute-start | bytes 3145736 | tf_op jit(solution)/shard_map/ppermute | solution.py:401
  59.4 0.0 collective-permute-start.15
  59.4 0.5 collective-permute-start.16
  59.9 0.0 collective-permute-start.17
  59.9 2.7 %collective-permute-start.18 = (bf16[128,1024]{1,0:T(8,128)(2,1)}, bf16[128,1024]{1,0:T(8,128)(2,1)S(1)}, u32[]{:S(2)}, u32[]{:S(2)}) collective-permute-start(bf16[128,1024]{1,0:T(8,128)(2,1)} %get-tuple-element.31.x_b), channel_id=1, source_target_pairs={{0,193},{1,0},{64,1},{65,64},{128,65},{129,128},{192,129},{193,192... | collective-permute-start | bytes 786440 | tf_op jit(solution)/shard_map/ppermute | solution.py:404
  62.6 0.1 pad_add_fusion.place
  62.7 6.6 %collective-permute-done.17.x_a = bf16[128,1024]{1,0:T(8,128)(2,1)S(1)} collective-permute-done((bf16[128,1024]{1,0:T(8,128)(2,1)}, bf16[128,1024]{1,0:T(8,128)(2,1)S(1)}, u32[]{:S(2)}, u32[]{:S(2)}) %collective-permute-start.17) | collective-permute-done | bytes 262176 | tf_op jit(solution)/shard_map/ppermute | solution.py:403
  69.3 0.0 collective-permute-done.18.x_b
  69.3 0.0 collective-permute-done.14.rest_5_
  69.3 0.0 collective-permute-done.15.rest_6_
  69.3 0.0 collective-permute-done.16.rest_7_
  69.3 5.6 %shard_map.116 = (bf16[128,1024]{1,0:T(8,128)(2,1)S(1)}, bf16[128,1024]{1,0:T(8,128)(2,1)S(1)}) custom-call(s32[3]{0:T(128)S(1)} %pad_add_fusion.place, bf16[128,1024]{1,0:T(8,128)(2,1)S(1)} %collective-permute-done.17.x_a, bf16[128,1024]{1,0:T(8,128)(2,1)S(1)} %collective-permute-done.18.x_b, bf16[4,2,32,2048]{3,2,1,0:T(8,128)(2,1)S(1)} %pad_maximum_fusion.rest_0_, ...), custom_call_target="tpu_custom_call" | custom-call | flops 2147483648 | bytes 10000000 | tf_op jit(solution)/shard_map/pallas_call | solution.py:334
  74.9 2.4 %collective-permute-start.19 = (bf16[128,1024]{1,0:T(8,128)(2,1)S(1)}, bf16[128,1024]{1,0:T(8,128)(2,1)S(1)}, u32[]{:S(2)}, u32[]{:S(2)}) collective-permute-start(bf16[128,1024]{1,0:T(8,128)(2,1)S(1)} %get-tuple-element.37), channel_id=1, source_target_pairs={{0,193},{1,0},{64,1},{65,64},{128,65},{129,128},{192,129},{193,192... | collective-permute-start | bytes 786440 | tf_op jit(solution)/shard_map/ppermute | solution.py:407
  77.3 0.0 collective-permute-start.20
  77.3 0.0 copy-done.1
  77.3 0.0 copy-done.2
  77.3 5.7 %shard_map.115 = (f32[128,1024]{1,0:T(8,128)S(1)}, f32[128,1024]{1,0:T(8,128)S(1)}) custom-call(s32[3]{0:T(128)S(1)} %pad_add_fusion.place, bf16[128,1024]{1,0:T(8,128)(2,1)S(1)} %copy-done.1, bf16[128,1024]{1,0:T(8,128)(2,1)S(1)} %copy-done.2, bf16[4,2,32,2048]{3,2,1,0:T(8,128)(2,1)S(1)} %pad_maximum_fusion.rest_0_, ...), custom_call_target="tpu_custom_call" | custom-call | flops 2147483648 | bytes 10000000 | tf_op jit(solution)/shard_map/pallas_call | solution.py:334
  83.1 0.0 collective-permute-done.19
  83.1 0.1 convert_add_fusion.1
  83.1 1.8 %collective-permute-done.20 = bf16[128,1024]{1,0:T(8,128)(2,1)S(1)} collective-permute-done((bf16[128,1024]{1,0:T(8,128)(2,1)S(1)}, bf16[128,1024]{1,0:T(8,128)(2,1)S(1)}, u32[]{:S(2)}, u32[]{:S(2)}) %collective-permute-start.20) | collective-permute-done | bytes 262176 | tf_op jit(solution)/shard_map/ppermute | solution.py:408
  84.9 0.1 convert_add_fusion
  85.0 1.0 %fusion = bf16[256,1024]{1,0:T(8,128)(2,1)} fusion(f32[128,1024]{1,0:T(8,128)S(1)} %convert_add_fusion, f32[128,1024]{1,0:T(8,128)S(1)} %convert_add_fusion.1, bf16[256,1024]{1,0:T(8,128)(2,1)S(1)} %copy-done.5), kind=kLoop, calls=%fused_computation.2 | loop fusion | flops 1048576 | bytes 2097152 | tf_op jit(solution)/shard_map/convert_element_type | solution.py:411
  (17 shorter events, 0.1 us)
Async XLA Ops:
  1.6 10.4 %collective-permute-start.6 = (bf16[32,2048]{1,0:T(8,128)(2,1)S(1)}, bf16[32,2048]{1,0:T(8,128)(2,1)S(1)}, u32[]{:S(2)}, u32[]{:S(2)}) collective-permute-start(bf16[32,2048]{1,0:T(8,128)(2,1)S(1)} %get-tuple-element.43), channel_id=1, source_target_pairs={{0,2},{2,0},{1,3},{3,1},{4,6},{6,4},{5,7},{7,5},{8,10},{10,8},{9,1... | collective-permute-start | bytes 393224 | tf_op jit(solution)/shard_map/ppermute | solution.py:378
  5.0 1.2 %copy-start = (bf16[16,64,512]{2,1,0:T(8,128)(2,1)S(1)}, bf16[16,64,512]{2,1,0:T(8,128)(2,1)}, u32[]{:S(2)}) copy-start(bf16[16,64,512]{2,1,0:T(8,128)(2,1)} %own_hbm.1) | copy-start | bytes 3145732
  6.2 0.7 copy-start.3
  7.0 24.0 %copy-start.4 = (bf16[16,128]{1,0:T(8,128)(2,1)}, bf16[16,128]{1,0:T(8,128)(2,1)S(1)}, u32[]{:S(2)}) copy-start(bf16[16,128]{1,0:T(8,128)(2,1)S(1)} %get-tuple-element.25.own_lab) | copy-start | bytes 12292
  7.0 8.0 %collective-permute-start.2 = (bf16[144,512]{1,0:T(8,128)(2,1)S(1)}, bf16[144,512]{1,0:T(8,128)(2,1)S(1)}, u32[]{:S(2)}, u32[]{:S(2)}) collective-permute-start(bf16[144,512]{1,0:T(8,128)(2,1)S(1)} %get-tuple-element.23), channel_id=1, source_target_pairs={{0,2},{2,4},{4,6},{6,8},{8,10},{10,12},{12,14},{14,16},{16,18},{18... | collective-permute-start | bytes 442376 | tf_op jit(solution)/shard_map/ppermute | solution.py:382
  7.1 8.8 %collective-permute-start.3 = (bf16[144,512]{1,0:T(8,128)(2,1)S(1)}, bf16[144,512]{1,0:T(8,128)(2,1)S(1)}, u32[]{:S(2)}, u32[]{:S(2)}) collective-permute-start(bf16[144,512]{1,0:T(8,128)(2,1)S(1)} %get-tuple-element.24), channel_id=1, source_target_pairs={{0,62},{2,0},{4,2},{6,4},{8,6},{10,8},{12,10},{14,12},{16,14},{18,... | collective-permute-start | bytes 442376 | tf_op jit(solution)/shard_map/ppermute | solution.py:383
  7.6 22.3 %collective-permute-start = (bf16[464,512]{1,0:T(8,128)(2,1)S(1)}, bf16[464,512]{1,0:T(8,128)(2,1)S(1)}, u32[]{:S(2)}, u32[]{:S(2)}) collective-permute-start(bf16[464,512]{1,0:T(8,128)(2,1)S(1)} %get-tuple-element.21), channel_id=1, source_target_pairs={{0,1},{1,64},{64,65},{65,128},{128,129},{129,192},{192,193},{193,0... | collective-permute-start | bytes 1425416 | tf_op jit(solution)/shard_map/ppermute | solution.py:380
  8.1 22.9 %collective-permute-start.1 = (bf16[464,512]{1,0:T(8,128)(2,1)S(1)}, bf16[464,512]{1,0:T(8,128)(2,1)S(1)}, u32[]{:S(2)}, u32[]{:S(2)}) collective-permute-start(bf16[464,512]{1,0:T(8,128)(2,1)S(1)} %get-tuple-element.22), channel_id=1, source_target_pairs={{0,193},{1,0},{64,1},{65,64},{128,65},{129,128},{192,129},{193,192... | collective-permute-start | bytes 1425416 | tf_op jit(solution)/shard_map/ppermute | solution.py:381
  12.1 6.8 %collective-permute-start.8 = (bf16[2,32,2048]{2,1,0:T(8,128)(2,1)S(1)}, bf16[2,32,2048]{2,1,0:T(8,128)(2,1)S(1)}, u32[]{:S(2)}, u32[]{:S(2)}) collective-permute-start(bf16[2,32,2048]{2,1,0:T(8,128)(2,1)S(1)} %get-tuple-element.41), channel_id=1, source_target_pairs={{8,0},{34,2},{12,4},{38,6},{0,8},{42,10},{4,12},{46,14},{24,16},{5... | collective-permute-start | bytes 786440 | tf_op jit(solution)/shard_map/ppermute | solution.py:362
  15.1 16.8 %copy-start.6 = (bf16[144,512]{1,0:T(8,128)(2,1)}, bf16[144,512]{1,0:T(8,128)(2,1)S(1)}, u32[]{:S(2)}) copy-start(bf16[144,512]{1,0:T(8,128)(2,1)S(1)} %collective-permute-done.2.left) | copy-start | bytes 442372
  15.1 7.3 %collective-permute-start.7 = (bf16[2,32,2048]{2,1,0:T(8,128)(2,1)S(1)}, bf16[2,32,2048]{2,1,0:T(8,128)(2,1)S(1)}, u32[]{:S(2)}, u32[]{:S(2)}) collective-permute-start(bf16[2,32,2048]{2,1,0:T(8,128)(2,1)S(1)} %get-tuple-element.41), channel_id=1, source_target_pairs={{4,0},{18,2},{8,4},{22,6},{12,8},{26,10},{0,12},{30,14},{20,16},{3... | collective-permute-start | bytes 786440 | tf_op jit(solution)/shard_map/ppermute | solution.py:362
  15.9 16.0 %copy-start.7 = (bf16[144,512]{1,0:T(8,128)(2,1)}, bf16[144,512]{1,0:T(8,128)(2,1)S(1)}, u32[]{:S(2)}) copy-start(bf16[144,512]{1,0:T(8,128)(2,1)S(1)} %collective-permute-done.3.right) | copy-start | bytes 442372
  15.9 6.8 %collective-permute-start.9 = (bf16[2,32,2048]{2,1,0:T(8,128)(2,1)S(1)}, bf16[2,32,2048]{2,1,0:T(8,128)(2,1)S(1)}, u32[]{:S(2)}, u32[]{:S(2)}) collective-permute-start(bf16[2,32,2048]{2,1,0:T(8,128)(2,1)S(1)} %get-tuple-element.41), channel_id=1, source_target_pairs={{12,0},{50,2},{0,4},{54,6},{4,8},{58,10},{8,12},{62,14},{28,16},{2... | collective-permute-start | bytes 786440 | tf_op jit(solution)/shard_map/ppermute | solution.py:362
  18.9 8.8 %collective-permute-start.5 = (bf16[128,512]{1,0:T(8,128)(2,1)S(1)}, bf16[128,512]{1,0:T(8,128)(2,1)S(1)}, u32[]{:S(2)}, u32[]{:S(2)}) collective-permute-start(bf16[128,512]{1,0:T(8,128)(2,1)S(1)} %get-tuple-element.48), channel_id=1, source_target_pairs={{0,193},{1,0},{64,1},{65,64},{128,65},{129,128},{192,129},{193,192... | collective-permute-start | bytes 393224 | tf_op jit(solution)/shard_map/ppermute | solution.py:390
  22.4 5.3 %collective-permute-start.4 = (bf16[128,512]{1,0:T(8,128)(2,1)S(1)}, bf16[128,512]{1,0:T(8,128)(2,1)S(1)}, u32[]{:S(2)}, u32[]{:S(2)}) collective-permute-start(bf16[128,512]{1,0:T(8,128)(2,1)S(1)} %get-tuple-element.49), channel_id=1, source_target_pairs={{0,1},{1,64},{64,65},{65,128},{128,129},{129,192},{192,193},{193,0... | collective-permute-start | bytes 393224 | tf_op jit(solution)/shard_map/ppermute | solution.py:387
  22.8 28.9 %collective-permute-start.13 = (bf16[4,2,32,2048]{3,2,1,0:T(8,128)(2,1)S(1)}, bf16[4,2,32,2048]{3,2,1,0:T(8,128)(2,1)}, u32[]{:S(2)}, u32[]{:S(2)}) collective-permute-start(bf16[4,2,32,2048]{3,2,1,0:T(8,128)(2,1)S(1)} %pad_maximum_fusion.rest_0_), channel_id=1, source_target_pairs={{0,2},{2,0},{1,3},{3,1},{4,6},{6,4},{5,7},{7,5},{8,10},{10,8},{9,1... | collective-permute-start | bytes 3145736 | tf_op jit(solution)/shard_map/ppermute | solution.py:395
  27.6 4.2 %copy-start.10 = (bf16[128,512]{1,0:T(8,128)(2,1)}, bf16[128,512]{1,0:T(8,128)(2,1)S(1)}, u32[]{:S(2)}) copy-start(bf16[128,512]{1,0:T(8,128)(2,1)S(1)} %collective-permute-done.5.down_c) | copy-start | bytes 393220
  27.6 26.5 %collective-permute-start.12 = (bf16[4,2,32,2048]{3,2,1,0:T(8,128)(2,1)S(1)}, bf16[4,2,32,2048]{3,2,1,0:T(8,128)(2,1)}, u32[]{:S(2)}, u32[]{:S(2)}) collective-permute-start(bf16[4,2,32,2048]{3,2,1,0:T(8,128)(2,1)S(1)} %pad_maximum_fusion.rest_0_), channel_id=1, source_target_pairs={{48,0},{14,2},{52,4},{2,6},{56,8},{6,10},{60,12},{10,14},{0,16},{3... | collective-permute-start | bytes 3145736 | tf_op jit(solution)/shard_map/ppermute | solution.py:362
  27.7 4.2 %copy-start.11 = (bf16[128,512]{1,0:T(8,128)(2,1)}, bf16[128,512]{1,0:T(8,128)(2,1)S(1)}, u32[]{:S(2)}) copy-start(bf16[128,512]{1,0:T(8,128)(2,1)S(1)} %collective-permute-done.4.up_c) | copy-start | bytes 393220
  27.7 26.5 %collective-permute-start.11 = (bf16[4,2,32,2048]{3,2,1,0:T(8,128)(2,1)S(1)}, bf16[4,2,32,2048]{3,2,1,0:T(8,128)(2,1)}, u32[]{:S(2)}, u32[]{:S(2)}) collective-permute-start(bf16[4,2,32,2048]{3,2,1,0:T(8,128)(2,1)S(1)} %pad_maximum_fusion.rest_0_), channel_id=1, source_target_pairs={{32,0},{10,2},{36,4},{14,6},{40,8},{2,10},{44,12},{6,14},{48,16},{... | collective-permute-start | bytes 3145736 | tf_op jit(solution)/shard_map/ppermute | solution.py:362
  29.9 2.0 %copy-start.8 = (bf16[464,512]{1,0:T(8,128)(2,1)}, bf16[464,512]{1,0:T(8,128)(2,1)S(1)}, u32[]{:S(2)}) copy-start(bf16[464,512]{1,0:T(8,128)(2,1)S(1)} %collective-permute-done.up) | copy-start | bytes 1425412
  29.9 24.9 %collective-permute-start.10 = (bf16[4,2,32,2048]{3,2,1,0:T(8,128)(2,1)S(1)}, bf16[4,2,32,2048]{3,2,1,0:T(8,128)(2,1)}, u32[]{:S(2)}, u32[]{:S(2)}) collective-permute-start(bf16[4,2,32,2048]{3,2,1,0:T(8,128)(2,1)S(1)} %pad_maximum_fusion.rest_0_), channel_id=1, source_target_pairs={{16,0},{6,2},{20,4},{10,6},{24,8},{14,10},{28,12},{2,14},{32,16},{... | collective-permute-start | bytes 3145736 | tf_op jit(solution)/shard_map/ppermute | solution.py:362
  31.0 0.8 copy-start.9
  54.8 14.5 %collective-permute-start.14 = (bf16[4,2,32,2048]{3,2,1,0:T(8,128)(2,1)}, bf16[4,2,32,2048]{3,2,1,0:T(8,128)(2,1)S(1)}, u32[]{:S(2)}, u32[]{:S(2)}) collective-permute-start(bf16[4,2,32,2048]{3,2,1,0:T(8,128)(2,1)} %collective-permute-done.10.rest_1_), channel_id=1, source_target_pairs={{0,2},{2,0},{1,3},{3,1},{4,6},{6,4},{5,7},{7,5},{8,10},{10,8},{9,1... | collective-permute-start | bytes 3145736 | tf_op jit(solution)/shard_map/ppermute | solution.py:401
  59.4 9.9 %collective-permute-start.15 = (bf16[4,2,32,2048]{3,2,1,0:T(8,128)(2,1)}, bf16[4,2,32,2048]{3,2,1,0:T(8,128)(2,1)}, u32[]{:S(2)}, u32[]{:S(2)}) collective-permute-start(bf16[4,2,32,2048]{3,2,1,0:T(8,128)(2,1)} %collective-permute-done.11.rest_2_), channel_id=1, source_target_pairs={{0,2},{2,0},{1,3},{3,1},{4,6},{6,4},{5,7},{7,5},{8,10},{10,8},{9,1... | collective-permute-start | bytes 3145736 | tf_op jit(solution)/shard_map/ppermute | solution.py:401
  59.4 9.9 %collective-permute-start.16 = (bf16[4,2,32,2048]{3,2,1,0:T(8,128)(2,1)}, bf16[4,2,32,2048]{3,2,1,0:T(8,128)(2,1)}, u32[]{:S(2)}, u32[]{:S(2)}) collective-permute-start(bf16[4,2,32,2048]{3,2,1,0:T(8,128)(2,1)} %collective-permute-done.12.rest_3_), channel_id=1, source_target_pairs={{0,2},{2,0},{1,3},{3,1},{4,6},{6,4},{5,7},{7,5},{8,10},{10,8},{9,1... | collective-permute-start | bytes 3145736 | tf_op jit(solution)/shard_map/ppermute | solution.py:401
  59.9 9.4 %collective-permute-start.17 = (bf16[128,1024]{1,0:T(8,128)(2,1)}, bf16[128,1024]{1,0:T(8,128)(2,1)S(1)}, u32[]{:S(2)}, u32[]{:S(2)}) collective-permute-start(bf16[128,1024]{1,0:T(8,128)(2,1)} %get-tuple-element.30.x_a), channel_id=1, source_target_pairs={{0,1},{1,64},{64,65},{65,128},{128,129},{129,192},{192,193},{193,0... | collective-permute-start | bytes 786440 | tf_op jit(solution)/shard_map/ppermute | solution.py:403
  59.9 9.4 %collective-permute-start.18 = (bf16[128,1024]{1,0:T(8,128)(2,1)}, bf16[128,1024]{1,0:T(8,128)(2,1)S(1)}, u32[]{:S(2)}, u32[]{:S(2)}) collective-permute-start(bf16[128,1024]{1,0:T(8,128)(2,1)} %get-tuple-element.31.x_b), channel_id=1, source_target_pairs={{0,193},{1,0},{64,1},{65,64},{128,65},{129,128},{192,129},{193,192... | collective-permute-start | bytes 786440 | tf_op jit(solution)/shard_map/ppermute | solution.py:404
  62.7 14.7 %copy-start.1 = (bf16[128,1024]{1,0:T(8,128)(2,1)S(1)}, bf16[128,1024]{1,0:T(8,128)(2,1)}, u32[]{:S(2)}) copy-start(bf16[128,1024]{1,0:T(8,128)(2,1)} %get-tuple-element.30.x_a) | copy-start | bytes 786436
  62.7 14.7 %copy-start.2 = (bf16[128,1024]{1,0:T(8,128)(2,1)S(1)}, bf16[128,1024]{1,0:T(8,128)(2,1)}, u32[]{:S(2)}) copy-start(bf16[128,1024]{1,0:T(8,128)(2,1)} %get-tuple-element.31.x_b) | copy-start | bytes 786436
  74.9 8.2 %collective-permute-start.19 = (bf16[128,1024]{1,0:T(8,128)(2,1)S(1)}, bf16[128,1024]{1,0:T(8,128)(2,1)S(1)}, u32[]{:S(2)}, u32[]{:S(2)}) collective-permute-start(bf16[128,1024]{1,0:T(8,128)(2,1)S(1)} %get-tuple-element.37), channel_id=1, source_target_pairs={{0,193},{1,0},{64,1},{65,64},{128,65},{129,128},{192,129},{193,192... | collective-permute-start | bytes 786440 | tf_op jit(solution)/shard_map/ppermute | solution.py:407
  77.3 7.7 %copy-start.5 = (bf16[256,1024]{1,0:T(8,128)(2,1)S(1)}, bf16[256,1024]{1,0:T(8,128)(2,1)}, u32[]{:S(2)}) copy-start(bf16[256,1024]{1,0:T(8,128)(2,1)} %get-tuple-element.27) | copy-start | bytes 1572868
  77.3 7.6 %collective-permute-start.20 = (bf16[128,1024]{1,0:T(8,128)(2,1)S(1)}, bf16[128,1024]{1,0:T(8,128)(2,1)S(1)}, u32[]{:S(2)}, u32[]{:S(2)}) collective-permute-start(bf16[128,1024]{1,0:T(8,128)(2,1)S(1)} %get-tuple-element.39), channel_id=1, source_target_pairs={{0,1},{1,64},{64,65},{65,128},{128,129},{129,192},{192,193},{193,0... | collective-permute-start | bytes 786440 | tf_op jit(solution)/shard_map/ppermute | solution.py:408

commit v4 on v3

--- a/solution.py
+++ b/solution.py
@@ -14,7 +14,7 @@
 CC = 1024
 BANDS = 3
 WINS = 9
-GROUP = 3
+GROUP = 9
 QUAD = 256
 MOST = 62 * 1024 * 1024
 COARSE_LIMIT = 32 * 1024 * 1024
@@ -71,7 +71,7 @@
     frame[24:31, 0] = down_v[0]
     frame[24:31, 9] = down_v[1]
 
-    @pl.loop(0, 7)
+    @pl.loop(0, 7, unroll=7)
     def _(r):
         at = pl.multiple_of(r * COLS, COLS)
         frame[1 + r, 1:9] = turned(up[pl.ds(at, COLS), :].astype(F32).reshape(8, 8, C), in_turn)
@@ -89,7 +89,7 @@
 
     copies[0].wait()
 
-    @pl.loop(0, ROWS)
+    @pl.loop(0, ROWS, unroll=4)
     def _(r):
         frame[8 + r, 1:9] = turned(own[r].astype(F32).reshape(8, 8, C), in_turn)
 
@@ -170,7 +170,7 @@
     copies[3].wait()
     out_sub = lax.broadcasted_iota(jnp.int32, (4, 8, 8, C), 2)
 
-    @pl.loop(0, ROWS // 4)
+    @pl.loop(0, ROWS // 4, unroll=2)
     def _(i):
         r = 4 * i
         across = mixed[pl.ds(8 - a + r, 4)]
@@ -184,7 +184,7 @@
         for t in range(4):
             fine[t, pl.ds(r, 4)] = exact[:, 128 * t : 128 * t + 128].reshape(4, COLS, 128)
 
-    @pl.loop(0, ROWS // 2)
+    @pl.loop(0, ROWS // 2, unroll=4)
     def _(i):
         parts = [
             fine[t, 2 * i + dr, pl.ds(dc, COLS // 2, stride=2), :]
@@ -390,6 +390,7 @@
     down_c = lax.ppermute(
         jnp.concatenate([left[:56], right[:56], side_lab]), rows_axes, ring(rows_n, -1)
     )
+    strip, up, down = lax.optimization_barrier((strip, up, down))
     zero, one, three, two = around(strip, True)
     far = [one, two, three]
     last = lax.ppermute(strip, "core", ring(2, 1))
@@ -397,7 +398,7 @@
         offsets, up, down, left, right, up_c, down_c, own_lab, tokens,
         norm_gain.reshape(1, -1), coarse_gain.reshape(1, -1), w_qkv, w_proj, w_merge,
     )
-    far, last, normed_a, normed_b = lax.optimization_barrier((far, last, normed_a, normed_b))
+    far, last, coarse = lax.optimization_barrier((far, last, coarse))
     swapped = [lax.ppermute(piece, "core", ring(2, 1)) for piece in far]
     pieces = [strip] + far + [last] + swapped
     their_a = lax.ppermute(normed_a, rows_axes, ring(rows_n, 1))

time: 86.6 us -> 83.5 us (0.964)
  waiting for transfers between devices: 14.3 us -> 20 us
  Pallas kernels: 31.4 us -> 26.5 us
  starting transfers between devices: 34.4 us -> 30.5 us
    ppermute x1, waiting for transfers between devices: 0.01 us -> 5.42 us  [on_device(): lax.ppermute(jnp.concatenate([left[72:128], right[72:128], side_lab]), ro...]
    pallas_call x1, Pallas kernels: 19.9 us -> 15 us  [fine_level(): pl.pallas_call(fine_kernel, out_shape=(jax.ShapeDtypeStruct((ROWS, COLS,...]
    ppermute x3, starting transfers between devices: 5.14 us -> 1.74 us  [on_device(): swapped = [lax.ppermute(piece, 'core', ring(2, 1)) for piece in far]]
  transfers between devices with their start and end apart: 21 -> 21, of which waited for: 7 -> 8; matrix products, arithmetic and copies ran while one was open for 0% -> 0% of each run, Pallas kernels for 30% -> 25%
where the time goes in v4:
time: 83.5 us; the launch traced here: 82.9 us
  starting transfers between devices  30.5 us (37%)
  Pallas kernels  26.5 us (32%)
  waiting for transfers between devices  20 us (24%)
  local copies, waits for them, and re-layouts  2.63 us (3%)
  other arithmetic  2.33 us (3%)
    pallas_call x1, Pallas kernels, fine_level(): pl.pallas_call(fine_kernel, out_shape=(jax.ShapeDtypeStruct((ROWS, COLS,...  15 us
    pallas_call x2, Pallas kernels, coarse_level(): pl.pallas_call(coarse_kernel, out_shape=(jax.ShapeDtypeStruct(x_a.shape,...  11.3 us
    ppermute x6, starting transfers between devices, from_ahead(): return lax.ppermute(block, ('y', 'x', 'core'), pairs)  7.22 us
    ppermute x1, waiting for transfers between devices, on_device(): their_a = lax.ppermute(normed_a, rows_axes, ring(rows_n, 1))  6.6 us
    ppermute x6, waiting for transfers between devices, from_ahead(): return lax.ppermute(block, ('y', 'x', 'core'), pairs)  6.15 us
    ppermute x1, waiting for transfers between devices, on_device(): lax.ppermute(jnp.concatenate([left[72:128], right[72:128], side_lab]), ro...  5.42 us
    ppermute x1, starting transfers between devices, on_device(): last = lax.ppermute(strip, 'core', ring(2, 1))  4.82 us
    ppermute x1, starting transfers between devices, on_device(): down = lax.ppermute(to_prev, rows_axes, ring(rows_n, -1))  3.94 us
  transfers between devices with their start and end apart: 21, of which 8 were waited for; matrix products, arithmetic and copies ran while one was open for 0% of the time, Pallas kernels for 25%

profile of v4, /device:TPU:1, one launch (start us, length us, event | category | flops | bytes accessed | tf_op | source)
XLA Modules:
  0.0 82.9 jit_solution(9126685743819098000)
XLA Ops:
  0.6 1.0 %fusion.1 = (bf16[1,32,2048]{2,1,0:T(8,128)(2,1)S(1)}, bf16[32,2048]{1,0:T(8,128)(2,1)S(1)}) fusion(bf16[32,2048]{1,0:T(8,128)(2,1)} %param.18, bf16[2048,32]{0,1:T(8,128)(2,1)} %param.19, pred[]{:T(512)S(6)} %eq.4), kind=kLoop, calls=%fused_computation.10 | loop fusion | flops 131072 | bytes 524289 | tf_op jit(solution)/shard_map/stack | solution.py:378
  1.6 3.3 %collective-permute-start = (bf16[32,2048]{1,0:T(8,128)(2,1)S(1)}, bf16[32,2048]{1,0:T(8,128)(2,1)S(1)}, u32[]{:S(2)}, u32[]{:S(2)}) collective-permute-start(bf16[32,2048]{1,0:T(8,128)(2,1)S(1)} %get-tuple-element.47), channel_id=1, source_target_pairs={{0,2},{2,0},{1,3},{3,1},{4,6},{6,4},{5,7},{7,5},{8,10},{10,8},{9,1... | collective-permute-start | bytes 393224 | tf_op jit(solution)/shard_map/ppermute | solution.py:378
  5.0 1.2 %copy-done = bf16[16,64,512]{2,1,0:T(8,128)(2,1)S(1)} copy-done((bf16[16,64,512]{2,1,0:T(8,128)(2,1)S(1)}, bf16[16,64,512]{2,1,0:T(8,128)(2,1)}, u32[]{:S(2)}) %copy-start) | copy-done | bytes 1048600
  6.2 0.7 copy-done.3
  6.9 0.1 shard_map.113
  7.0 0.0 collective-permute-start.6
  7.1 0.5 collective-permute-start.7
  7.6 0.5 collective-permute-start.4
  8.1 3.9 %collective-permute-start.5 = (bf16[464,512]{1,0:T(8,128)(2,1)S(1)}, bf16[464,512]{1,0:T(8,128)(2,1)S(1)}, u32[]{:S(2)}, u32[]{:S(2)}) collective-permute-start(bf16[464,512]{1,0:T(8,128)(2,1)S(1)} %get-tuple-element.24), channel_id=1, source_target_pairs={{0,193},{1,0},{64,1},{65,64},{128,65},{129,128},{192,129},{193,192... | collective-permute-start | bytes 1425416 | tf_op jit(solution)/shard_map/ppermute | solution.py:381
  12.0 0.0 collective-permute-done
  12.1 3.0 %collective-permute-start.2 = (bf16[2,32,2048]{2,1,0:T(8,128)(2,1)S(1)}, bf16[2,32,2048]{2,1,0:T(8,128)(2,1)S(1)}, u32[]{:S(2)}, u32[]{:S(2)}) collective-permute-start(bf16[2,32,2048]{2,1,0:T(8,128)(2,1)S(1)} %get-tuple-element.45), channel_id=1, source_target_pairs={{8,0},{34,2},{12,4},{38,6},{0,8},{42,10},{4,12},{46,14},{24,16},{5... | collective-permute-start | bytes 786440 | tf_op jit(solution)/shard_map/ppermute | solution.py:362
  15.1 0.0 collective-permute-done.6.left
  15.1 0.8 collective-permute-start.1
  15.9 0.0 collective-permute-done.7.right
  15.9 0.0 copy-start.7
  15.9 0.8 collective-permute-start.3
  16.7 2.2 %collective-permute-done.2 = bf16[2,32,2048]{2,1,0:T(8,128)(2,1)S(1)} collective-permute-done((bf16[2,32,2048]{2,1,0:T(8,128)(2,1)S(1)}, bf16[2,32,2048]{2,1,0:T(8,128)(2,1)S(1)}, u32[]{:S(2)}, u32[]{:S(2)}) %collective-permute-start.2) | collective-permute-done | bytes 262176 | tf_op jit(solution)/shard_map/ppermute | solution.py:362
  18.9 3.1 %collective-permute-start.9 = (bf16[128,512]{1,0:T(8,128)(2,1)S(1)}, bf16[128,512]{1,0:T(8,128)(2,1)S(1)}, u32[]{:S(2)}, u32[]{:S(2)}) collective-permute-start(bf16[128,512]{1,0:T(8,128)(2,1)S(1)} %get-tuple-element.52), channel_id=1, source_target_pairs={{0,193},{1,0},{64,1},{65,64},{128,65},{129,128},{192,129},{193,192... | collective-permute-start | bytes 393224 | tf_op jit(solution)/shard_map/ppermute | solution.py:390
  22.0 0.4 collective-permute-done.1
  22.4 0.3 collective-permute-done.3
  22.7 0.1 pad_maximum_fusion.rest_0_
  22.8 0.0 collective-permute-done.4.up
  22.8 0.0 copy-start.8
  22.8 0.0 collective-permute-done.5.down
  22.9 0.0 copy-start.9
  22.9 4.8 %collective-permute-start.13 = (bf16[4,2,32,2048]{3,2,1,0:T(8,128)(2,1)S(1)}, bf16[4,2,32,2048]{3,2,1,0:T(8,128)(2,1)}, u32[]{:S(2)}, u32[]{:S(2)}) collective-permute-start(bf16[4,2,32,2048]{3,2,1,0:T(8,128)(2,1)S(1)} %pad_maximum_fusion.rest_0_), channel_id=1, source_target_pairs={{0,2},{2,0},{1,3},{3,1},{4,6},{6,4},{5,7},{7,5},{8,10},{10,8},{9,1... | collective-permute-start | bytes 3145736 | tf_op jit(solution)/shard_map/ppermute | solution.py:396
  27.7 0.0 collective-permute-start.12
  27.7 0.0 copy-done.4
  27.7 1.5 %collective-permute-start.11 = (bf16[4,2,32,2048]{3,2,1,0:T(8,128)(2,1)S(1)}, bf16[4,2,32,2048]{3,2,1,0:T(8,128)(2,1)}, u32[]{:S(2)}, u32[]{:S(2)}) collective-permute-start(bf16[4,2,32,2048]{3,2,1,0:T(8,128)(2,1)S(1)} %pad_maximum_fusion.rest_0_), channel_id=1, source_target_pairs={{32,0},{10,2},{36,4},{14,6},{40,8},{2,10},{44,12},{6,14},{48,16},{... | collective-permute-start | bytes 3145736 | tf_op jit(solution)/shard_map/ppermute | solution.py:362
  29.2 1.2 %collective-permute-start.10 = (bf16[4,2,32,2048]{3,2,1,0:T(8,128)(2,1)S(1)}, bf16[4,2,32,2048]{3,2,1,0:T(8,128)(2,1)}, u32[]{:S(2)}, u32[]{:S(2)}) collective-permute-start(bf16[4,2,32,2048]{3,2,1,0:T(8,128)(2,1)S(1)} %pad_maximum_fusion.rest_0_), channel_id=1, source_target_pairs={{16,0},{6,2},{20,4},{10,6},{24,8},{14,10},{28,12},{2,14},{32,16},{... | collective-permute-start | bytes 3145736 | tf_op jit(solution)/shard_map/ppermute | solution.py:362
  30.4 0.0 collective-permute-done.9.down_c
  30.4 0.0 collective-permute-start.8
  30.4 5.4 %collective-permute-done.8.up_c = bf16[128,512]{1,0:T(8,128)(2,1)S(1)} collective-permute-done((bf16[128,512]{1,0:T(8,128)(2,1)S(1)}, bf16[128,512]{1,0:T(8,128)(2,1)S(1)}, u32[]{:S(2)}, u32[]{:S(2)}) %collective-permute-start.8) | collective-permute-done | bytes 131104 | tf_op jit(solution)/shard_map/ppermute | solution.py:387
  35.8 0.0 copy-done.9
  35.8 0.7 copy-done.11
  36.5 0.0 copy-done.6
  36.5 0.0 copy-done.7
  36.5 0.0 copy-done.8
  36.5 0.0 copy-done.10
  36.5 15.0 %shard_map.114 = (bf16[16,64,512]{2,1,0:T(8,128)(2,1)}, bf16[256,1024]{1,0:T(8,128)(2,1)}, bf16[128,1024]{1,0:T(8,128)(2,1)}, bf16[128,1024]{1,0:T(8,128)(2,1)}) custom-call(s32[2]{0:T(128)} %offs.1, bf16[464,512]{1,0:T(8,128)(2,1)} %copy-done.8, bf16[464,512]{1,0:T(8,128)(2,1)} %copy-done.9, bf16[144,512]{1,0:T(8,128)(2,1)} %copy-done.6, ...), custom_call_target="tpu_custom_call" | custom-call | flops 8999999488 | bytes 12000000 | tf_op jit(solution)/shard_map/pallas_call | solution.py:256
  51.5 0.0 collective-permute-done.13.rest_4_
  51.5 2.7 %collective-permute-done.12.rest_3_ = bf16[4,2,32,2048]{3,2,1,0:T(8,128)(2,1)} collective-permute-done((bf16[4,2,32,2048]{3,2,1,0:T(8,128)(2,1)S(1)}, bf16[4,2,32,2048]{3,2,1,0:T(8,128)(2,1)}, u32[]{:S(2)}, u32[]{:S(2)}) %collective-permute-start.12) | collective-permute-done | bytes 1048608 | tf_op jit(solution)/shard_map/ppermute | solution.py:362
  54.2 0.0 collective-permute-done.11.rest_2_
  54.2 0.6 collective-permute-done.10.rest_1_
  54.8 1.2 %collective-permute-start.14 = (bf16[4,2,32,2048]{3,2,1,0:T(8,128)(2,1)}, bf16[4,2,32,2048]{3,2,1,0:T(8,128)(2,1)S(1)}, u32[]{:S(2)}, u32[]{:S(2)}) collective-permute-start(bf16[4,2,32,2048]{3,2,1,0:T(8,128)(2,1)} %collective-permute-done.10.rest_1_), channel_id=1, source_target_pairs={{0,2},{2,0},{1,3},{3,1},{4,6},{6,4},{5,7},{7,5},{8,10},{10,8},{9,1... | collective-permute-start | bytes 3145736 | tf_op jit(solution)/shard_map/ppermute | solution.py:402
  56.0 0.0 collective-permute-start.15
  56.0 0.5 collective-permute-start.16
  56.5 0.0 collective-permute-start.17
  56.5 2.7 %collective-permute-start.18 = (bf16[128,1024]{1,0:T(8,128)(2,1)}, bf16[128,1024]{1,0:T(8,128)(2,1)S(1)}, u32[]{:S(2)}, u32[]{:S(2)}) collective-permute-start(bf16[128,1024]{1,0:T(8,128)(2,1)} %get-tuple-element.35.x_b), channel_id=1, source_target_pairs={{0,193},{1,0},{64,1},{65,64},{128,65},{129,128},{192,129},{193,192... | collective-permute-start | bytes 786440 | tf_op jit(solution)/shard_map/ppermute | solution.py:405
  59.2 0.1 pad_add_fusion.place
  59.3 6.6 %collective-permute-done.17.x_a = bf16[128,1024]{1,0:T(8,128)(2,1)S(1)} collective-permute-done((bf16[128,1024]{1,0:T(8,128)(2,1)}, bf16[128,1024]{1,0:T(8,128)(2,1)S(1)}, u32[]{:S(2)}, u32[]{:S(2)}) %collective-permute-start.17) | collective-permute-done | bytes 262176 | tf_op jit(solution)/shard_map/ppermute | solution.py:404
  65.9 0.0 collective-permute-done.18.x_b
  65.9 0.0 collective-permute-done.14.rest_5_
  65.9 0.0 collective-permute-done.15.rest_6_
  65.9 0.0 collective-permute-done.16.rest_7_
  65.9 5.6 %shard_map.116 = (bf16[128,1024]{1,0:T(8,128)(2,1)S(1)}, bf16[128,1024]{1,0:T(8,128)(2,1)S(1)}) custom-call(s32[3]{0:T(128)S(1)} %pad_add_fusion.place, bf16[128,1024]{1,0:T(8,128)(2,1)S(1)} %collective-permute-done.17.x_a, bf16[128,1024]{1,0:T(8,128)(2,1)S(1)} %collective-permute-done.18.x_b, bf16[4,2,32,2048]{3,2,1,0:T(8,128)(2,1)S(1)} %pad_maximum_fusion.rest_0_, ...), custom_call_target="tpu_custom_call" | custom-call | flops 2147483648 | bytes 10000000 | tf_op jit(solution)/shard_map/pallas_call | solution.py:334
  71.5 2.6 %collective-permute-start.19 = (bf16[128,1024]{1,0:T(8,128)(2,1)S(1)}, bf16[128,1024]{1,0:T(8,128)(2,1)S(1)}, u32[]{:S(2)}, u32[]{:S(2)}) collective-permute-start(bf16[128,1024]{1,0:T(8,128)(2,1)S(1)} %get-tuple-element.41), channel_id=1, source_target_pairs={{0,193},{1,0},{64,1},{65,64},{128,65},{129,128},{192,129},{193,192... | collective-permute-start | bytes 786440 | tf_op jit(solution)/shard_map/ppermute | solution.py:408
  74.2 0.0 collective-permute-start.20
  74.2 5.7 %shard_map.115 = (f32[128,1024]{1,0:T(8,128)S(1)}, f32[128,1024]{1,0:T(8,128)S(1)}) custom-call(s32[3]{0:T(128)S(1)} %pad_add_fusion.place, bf16[128,1024]{1,0:T(8,128)(2,1)S(1)} %copy-done.1, bf16[128,1024]{1,0:T(8,128)(2,1)S(1)} %copy-done.2, bf16[4,2,32,2048]{3,2,1,0:T(8,128)(2,1)S(1)} %pad_maximum_fusion.rest_0_, ...), custom_call_target="tpu_custom_call" | custom-call | flops 2147483648 | bytes 10000000 | tf_op jit(solution)/shard_map/pallas_call | solution.py:334
  79.9 0.0 collective-permute-done.19
  79.9 0.1 convert_add_fusion.1
  80.0 1.8 %collective-permute-done.20 = bf16[128,1024]{1,0:T(8,128)(2,1)S(1)} collective-permute-done((bf16[128,1024]{1,0:T(8,128)(2,1)S(1)}, bf16[128,1024]{1,0:T(8,128)(2,1)S(1)}, u32[]{:S(2)}, u32[]{:S(2)}) %collective-permute-start.20) | collective-permute-done | bytes 262176 | tf_op jit(solution)/shard_map/ppermute | solution.py:409
  81.8 0.1 convert_add_fusion
  81.9 1.0 %fusion = bf16[256,1024]{1,0:T(8,128)(2,1)} fusion(f32[128,1024]{1,0:T(8,128)S(1)} %convert_add_fusion, f32[128,1024]{1,0:T(8,128)S(1)} %convert_add_fusion.1, bf16[256,1024]{1,0:T(8,128)(2,1)S(1)} %copy-done.5), kind=kLoop, calls=%fused_computation.2 | loop fusion | flops 1048576 | bytes 2097152 | tf_op jit(solution)/shard_map/convert_element_type | solution.py:412
  (17 shorter events, 0.1 us)
Async XLA Ops:
  1.6 10.4 %collective-permute-start = (bf16[32,2048]{1,0:T(8,128)(2,1)S(1)}, bf16[32,2048]{1,0:T(8,128)(2,1)S(1)}, u32[]{:S(2)}, u32[]{:S(2)}) collective-permute-start(bf16[32,2048]{1,0:T(8,128)(2,1)S(1)} %get-tuple-element.47), channel_id=1, source_target_pairs={{0,2},{2,0},{1,3},{3,1},{4,6},{6,4},{5,7},{7,5},{8,10},{10,8},{9,1... | collective-permute-start | bytes 393224 | tf_op jit(solution)/shard_map/ppermute | solution.py:378
  5.0 1.2 %copy-start = (bf16[16,64,512]{2,1,0:T(8,128)(2,1)S(1)}, bf16[16,64,512]{2,1,0:T(8,128)(2,1)}, u32[]{:S(2)}) copy-start(bf16[16,64,512]{2,1,0:T(8,128)(2,1)} %own_hbm.1) | copy-start | bytes 3145732
  6.2 0.7 copy-start.3
  7.0 20.7 %copy-start.4 = (bf16[16,128]{1,0:T(8,128)(2,1)}, bf16[16,128]{1,0:T(8,128)(2,1)S(1)}, u32[]{:S(2)}) copy-start(bf16[16,128]{1,0:T(8,128)(2,1)S(1)} %get-tuple-element.29.own_lab) | copy-start | bytes 12292
  7.0 8.0 %collective-permute-start.6 = (bf16[144,512]{1,0:T(8,128)(2,1)S(1)}, bf16[144,512]{1,0:T(8,128)(2,1)S(1)}, u32[]{:S(2)}, u32[]{:S(2)}) collective-permute-start(bf16[144,512]{1,0:T(8,128)(2,1)S(1)} %get-tuple-element.27), channel_id=1, source_target_pairs={{0,2},{2,4},{4,6},{6,8},{8,10},{10,12},{12,14},{14,16},{16,18},{18... | collective-permute-start | bytes 442376 | tf_op jit(solution)/shard_map/ppermute | solution.py:382
  7.1 8.8 %collective-permute-start.7 = (bf16[144,512]{1,0:T(8,128)(2,1)S(1)}, bf16[144,512]{1,0:T(8,128)(2,1)S(1)}, u32[]{:S(2)}, u32[]{:S(2)}) collective-permute-start(bf16[144,512]{1,0:T(8,128)(2,1)S(1)} %get-tuple-element.28), channel_id=1, source_target_pairs={{0,62},{2,0},{4,2},{6,4},{8,6},{10,8},{12,10},{14,12},{16,14},{18,... | collective-permute-start | bytes 442376 | tf_op jit(solution)/shard_map/ppermute | solution.py:383
  7.6 15.3 %collective-permute-start.4 = (bf16[464,512]{1,0:T(8,128)(2,1)S(1)}, bf16[464,512]{1,0:T(8,128)(2,1)S(1)}, u32[]{:S(2)}, u32[]{:S(2)}) collective-permute-start(bf16[464,512]{1,0:T(8,128)(2,1)S(1)} %get-tuple-element.23), channel_id=1, source_target_pairs={{0,1},{1,64},{64,65},{65,128},{128,129},{129,192},{192,193},{193,0... | collective-permute-start | bytes 1425416 | tf_op jit(solution)/shard_map/ppermute | solution.py:380
  8.1 14.8 %collective-permute-start.5 = (bf16[464,512]{1,0:T(8,128)(2,1)S(1)}, bf16[464,512]{1,0:T(8,128)(2,1)S(1)}, u32[]{:S(2)}, u32[]{:S(2)}) collective-permute-start(bf16[464,512]{1,0:T(8,128)(2,1)S(1)} %get-tuple-element.24), channel_id=1, source_target_pairs={{0,193},{1,0},{64,1},{65,64},{128,65},{129,128},{192,129},{193,192... | collective-permute-start | bytes 1425416 | tf_op jit(solution)/shard_map/ppermute | solution.py:381
  12.1 6.8 %collective-permute-start.2 = (bf16[2,32,2048]{2,1,0:T(8,128)(2,1)S(1)}, bf16[2,32,2048]{2,1,0:T(8,128)(2,1)S(1)}, u32[]{:S(2)}, u32[]{:S(2)}) collective-permute-start(bf16[2,32,2048]{2,1,0:T(8,128)(2,1)S(1)} %get-tuple-element.45), channel_id=1, source_target_pairs={{8,0},{34,2},{12,4},{38,6},{0,8},{42,10},{4,12},{46,14},{24,16},{5... | collective-permute-start | bytes 786440 | tf_op jit(solution)/shard_map/ppermute | solution.py:362
  15.1 21.4 %copy-start.6 = (bf16[144,512]{1,0:T(8,128)(2,1)}, bf16[144,512]{1,0:T(8,128)(2,1)S(1)}, u32[]{:S(2)}) copy-start(bf16[144,512]{1,0:T(8,128)(2,1)S(1)} %collective-permute-done.6.left) | copy-start | bytes 442372
  15.1 7.3 %collective-permute-start.1 = (bf16[2,32,2048]{2,1,0:T(8,128)(2,1)S(1)}, bf16[2,32,2048]{2,1,0:T(8,128)(2,1)S(1)}, u32[]{:S(2)}, u32[]{:S(2)}) collective-permute-start(bf16[2,32,2048]{2,1,0:T(8,128)(2,1)S(1)} %get-tuple-element.45), channel_id=1, source_target_pairs={{4,0},{18,2},{8,4},{22,6},{12,8},{26,10},{0,12},{30,14},{20,16},{3... | collective-permute-start | bytes 786440 | tf_op jit(solution)/shard_map/ppermute | solution.py:362
  15.9 20.6 %copy-start.7 = (bf16[144,512]{1,0:T(8,128)(2,1)}, bf16[144,512]{1,0:T(8,128)(2,1)S(1)}, u32[]{:S(2)}) copy-start(bf16[144,512]{1,0:T(8,128)(2,1)S(1)} %collective-permute-done.7.right) | copy-start | bytes 442372
  15.9 6.8 %collective-permute-start.3 = (bf16[2,32,2048]{2,1,0:T(8,128)(2,1)S(1)}, bf16[2,32,2048]{2,1,0:T(8,128)(2,1)S(1)}, u32[]{:S(2)}, u32[]{:S(2)}) collective-permute-start(bf16[2,32,2048]{2,1,0:T(8,128)(2,1)S(1)} %get-tuple-element.45), channel_id=1, source_target_pairs={{12,0},{50,2},{0,4},{54,6},{4,8},{58,10},{8,12},{62,14},{28,16},{2... | collective-permute-start | bytes 786440 | tf_op jit(solution)/shard_map/ppermute | solution.py:362
  18.9 11.5 %collective-permute-start.9 = (bf16[128,512]{1,0:T(8,128)(2,1)S(1)}, bf16[128,512]{1,0:T(8,128)(2,1)S(1)}, u32[]{:S(2)}, u32[]{:S(2)}) collective-permute-start(bf16[128,512]{1,0:T(8,128)(2,1)S(1)} %get-tuple-element.52), channel_id=1, source_target_pairs={{0,193},{1,0},{64,1},{65,64},{128,65},{129,128},{192,129},{193,192... | collective-permute-start | bytes 393224 | tf_op jit(solution)/shard_map/ppermute | solution.py:390
  22.8 13.6 %copy-start.8 = (bf16[464,512]{1,0:T(8,128)(2,1)}, bf16[464,512]{1,0:T(8,128)(2,1)S(1)}, u32[]{:S(2)}) copy-start(bf16[464,512]{1,0:T(8,128)(2,1)S(1)} %collective-permute-done.4.up) | copy-start | bytes 1425412
  22.9 12.9 %copy-start.9 = (bf16[464,512]{1,0:T(8,128)(2,1)}, bf16[464,512]{1,0:T(8,128)(2,1)S(1)}, u32[]{:S(2)}) copy-start(bf16[464,512]{1,0:T(8,128)(2,1)S(1)} %collective-permute-done.5.down) | copy-start | bytes 1425412
  22.9 28.6 %collective-permute-start.13 = (bf16[4,2,32,2048]{3,2,1,0:T(8,128)(2,1)S(1)}, bf16[4,2,32,2048]{3,2,1,0:T(8,128)(2,1)}, u32[]{:S(2)}, u32[]{:S(2)}) collective-permute-start(bf16[4,2,32,2048]{3,2,1,0:T(8,128)(2,1)S(1)} %pad_maximum_fusion.rest_0_), channel_id=1, source_target_pairs={{0,2},{2,0},{1,3},{3,1},{4,6},{6,4},{5,7},{7,5},{8,10},{10,8},{9,1... | collective-permute-start | bytes 3145736 | tf_op jit(solution)/shard_map/ppermute | solution.py:396
  27.7 26.5 %collective-permute-start.12 = (bf16[4,2,32,2048]{3,2,1,0:T(8,128)(2,1)S(1)}, bf16[4,2,32,2048]{3,2,1,0:T(8,128)(2,1)}, u32[]{:S(2)}, u32[]{:S(2)}) collective-permute-start(bf16[4,2,32,2048]{3,2,1,0:T(8,128)(2,1)S(1)} %pad_maximum_fusion.rest_0_), channel_id=1, source_target_pairs={{48,0},{14,2},{52,4},{2,6},{56,8},{6,10},{60,12},{10,14},{0,16},{3... | collective-permute-start | bytes 3145736 | tf_op jit(solution)/shard_map/ppermute | solution.py:362
  27.7 26.5 %collective-permute-start.11 = (bf16[4,2,32,2048]{3,2,1,0:T(8,128)(2,1)S(1)}, bf16[4,2,32,2048]{3,2,1,0:T(8,128)(2,1)}, u32[]{:S(2)}, u32[]{:S(2)}) collective-permute-start(bf16[4,2,32,2048]{3,2,1,0:T(8,128)(2,1)S(1)} %pad_maximum_fusion.rest_0_), channel_id=1, source_target_pairs={{32,0},{10,2},{36,4},{14,6},{40,8},{2,10},{44,12},{6,14},{48,16},{... | collective-permute-start | bytes 3145736 | tf_op jit(solution)/shard_map/ppermute | solution.py:362
  29.2 25.6 %collective-permute-start.10 = (bf16[4,2,32,2048]{3,2,1,0:T(8,128)(2,1)S(1)}, bf16[4,2,32,2048]{3,2,1,0:T(8,128)(2,1)}, u32[]{:S(2)}, u32[]{:S(2)}) collective-permute-start(bf16[4,2,32,2048]{3,2,1,0:T(8,128)(2,1)S(1)} %pad_maximum_fusion.rest_0_), channel_id=1, source_target_pairs={{16,0},{6,2},{20,4},{10,6},{24,8},{14,10},{28,12},{2,14},{32,16},{... | collective-permute-start | bytes 3145736 | tf_op jit(solution)/shard_map/ppermute | solution.py:362
  30.4 6.1 %copy-start.10 = (bf16[128,512]{1,0:T(8,128)(2,1)}, bf16[128,512]{1,0:T(8,128)(2,1)S(1)}, u32[]{:S(2)}) copy-start(bf16[128,512]{1,0:T(8,128)(2,1)S(1)} %collective-permute-done.9.down_c) | copy-start | bytes 393220
  30.4 5.4 %collective-permute-start.8 = (bf16[128,512]{1,0:T(8,128)(2,1)S(1)}, bf16[128,512]{1,0:T(8,128)(2,1)S(1)}, u32[]{:S(2)}, u32[]{:S(2)}) collective-permute-start(bf16[128,512]{1,0:T(8,128)(2,1)S(1)} %get-tuple-element.53), channel_id=1, source_target_pairs={{0,1},{1,64},{64,65},{65,128},{128,129},{129,192},{192,193},{193,0... | collective-permute-start | bytes 393224 | tf_op jit(solution)/shard_map/ppermute | solution.py:387
  35.8 0.7 copy-start.11
  54.8 11.1 %collective-permute-start.14 = (bf16[4,2,32,2048]{3,2,1,0:T(8,128)(2,1)}, bf16[4,2,32,2048]{3,2,1,0:T(8,128)(2,1)S(1)}, u32[]{:S(2)}, u32[]{:S(2)}) collective-permute-start(bf16[4,2,32,2048]{3,2,1,0:T(8,128)(2,1)} %collective-permute-done.10.rest_1_), channel_id=1, source_target_pairs={{0,2},{2,0},{1,3},{3,1},{4,6},{6,4},{5,7},{7,5},{8,10},{10,8},{9,1... | collective-permute-start | bytes 3145736 | tf_op jit(solution)/shard_map/ppermute | solution.py:402
  56.0 9.9 %collective-permute-start.15 = (bf16[4,2,32,2048]{3,2,1,0:T(8,128)(2,1)}, bf16[4,2,32,2048]{3,2,1,0:T(8,128)(2,1)}, u32[]{:S(2)}, u32[]{:S(2)}) collective-permute-start(bf16[4,2,32,2048]{3,2,1,0:T(8,128)(2,1)} %collective-permute-done.11.rest_2_), channel_id=1, source_target_pairs={{0,2},{2,0},{1,3},{3,1},{4,6},{6,4},{5,7},{7,5},{8,10},{10,8},{9,1... | collective-permute-start | bytes 3145736 | tf_op jit(solution)/shard_map/ppermute | solution.py:402
  56.0 9.9 %collective-permute-start.16 = (bf16[4,2,32,2048]{3,2,1,0:T(8,128)(2,1)}, bf16[4,2,32,2048]{3,2,1,0:T(8,128)(2,1)}, u32[]{:S(2)}, u32[]{:S(2)}) collective-permute-start(bf16[4,2,32,2048]{3,2,1,0:T(8,128)(2,1)} %collective-permute-done.12.rest_3_), channel_id=1, source_target_pairs={{0,2},{2,0},{1,3},{3,1},{4,6},{6,4},{5,7},{7,5},{8,10},{10,8},{9,1... | collective-permute-start | bytes 3145736 | tf_op jit(solution)/shard_map/ppermute | solution.py:402
  56.5 9.4 %collective-permute-start.17 = (bf16[128,1024]{1,0:T(8,128)(2,1)}, bf16[128,1024]{1,0:T(8,128)(2,1)S(1)}, u32[]{:S(2)}, u32[]{:S(2)}) collective-permute-start(bf16[128,1024]{1,0:T(8,128)(2,1)} %get-tuple-element.34.x_a), channel_id=1, source_target_pairs={{0,1},{1,64},{64,65},{65,128},{128,129},{129,192},{192,193},{193,0... | collective-permute-start | bytes 786440 | tf_op jit(solution)/shard_map/ppermute | solution.py:404
  56.5 9.4 %collective-permute-start.18 = (bf16[128,1024]{1,0:T(8,128)(2,1)}, bf16[128,1024]{1,0:T(8,128)(2,1)S(1)}, u32[]{:S(2)}, u32[]{:S(2)}) collective-permute-start(bf16[128,1024]{1,0:T(8,128)(2,1)} %get-tuple-element.35.x_b), channel_id=1, source_target_pairs={{0,193},{1,0},{64,1},{65,64},{128,65},{129,128},{192,129},{193,192... | collective-permute-start | bytes 786440 | tf_op jit(solution)/shard_map/ppermute | solution.py:405
  59.3 14.9 %copy-start.1 = (bf16[128,1024]{1,0:T(8,128)(2,1)S(1)}, bf16[128,1024]{1,0:T(8,128)(2,1)}, u32[]{:S(2)}) copy-start(bf16[128,1024]{1,0:T(8,128)(2,1)} %get-tuple-element.34.x_a) | copy-start | bytes 786436
  59.3 14.9 %copy-start.2 = (bf16[128,1024]{1,0:T(8,128)(2,1)S(1)}, bf16[128,1024]{1,0:T(8,128)(2,1)}, u32[]{:S(2)}) copy-start(bf16[128,1024]{1,0:T(8,128)(2,1)} %get-tuple-element.35.x_b) | copy-start | bytes 786436
  71.5 8.4 %collective-permute-start.19 = (bf16[128,1024]{1,0:T(8,128)(2,1)S(1)}, bf16[128,1024]{1,0:T(8,128)(2,1)S(1)}, u32[]{:S(2)}, u32[]{:S(2)}) collective-permute-start(bf16[128,1024]{1,0:T(8,128)(2,1)S(1)} %get-tuple-element.41), channel_id=1, source_target_pairs={{0,193},{1,0},{64,1},{65,64},{128,65},{129,128},{192,129},{193,192... | collective-permute-start | bytes 786440 | tf_op jit(solution)/shard_map/ppermute | solution.py:408
  74.2 7.7 %copy-start.5 = (bf16[256,1024]{1,0:T(8,128)(2,1)S(1)}, bf16[256,1024]{1,0:T(8,128)(2,1)}, u32[]{:S(2)}) copy-start(bf16[256,1024]{1,0:T(8,128)(2,1)} %get-tuple-element.33) | copy-start | bytes 1572868
  74.2 7.6 %collective-permute-start.20 = (bf16[128,1024]{1,0:T(8,128)(2,1)S(1)}, bf16[128,1024]{1,0:T(8,128)(2,1)S(1)}, u32[]{:S(2)}, u32[]{:S(2)}) collective-permute-start(bf16[128,1024]{1,0:T(8,128)(2,1)S(1)} %get-tuple-element.43), channel_id=1, source_target_pairs={{0,1},{1,64},{64,65},{65,128},{128,129},{129,192},{192,193},{193,0... | collective-permute-start | bytes 786440 | tf_op jit(solution)/shard_map/ppermute | solution.py:409
